TPU v7x, 512 devices: a whole 4x8x8 slice. The times are simulated.
512 devices in a mesh: row: 32 (over z_hi, y), col: 16 (over z_lo, x, core).
Axes of the slice: x: 4, y: 8, z: 8 (z_hi: 4, z_lo: 2; z = z_hi * 2 + z_lo), core: 2. Of those that a mesh axis runs over, the one named last changes fastest.
Arguments:
- probes: bfloat16 [524288, 64], P(('row', 'col')), may hold values from -2 to 2
- points: bfloat16 [3, 524288], P(None, ('row', 'col')), may hold values from 0 to 1
- skeleton: bfloat16 [3, 229376], P(None, ('row', 'col')), may hold values from 0 to 1
- leaf_basis: bfloat16 [524288, 64], P(('row', 'col')), may hold values from -0.375 to 0.375
- transfer: bfloat16 [196608, 64], P(('row', 'col')), may hold values from -0.75 to 0.75
- near_list: int32 [32, 16, 2, 64], P('row', 'col'), may hold values from 0 to 127, as said below
- near_count: int32 [32, 16], P('row', 'col'), may hold values from 8 to 64, as said below
- far_list: int32 [32, 16, 2, 128], P('row', 'col'), may hold values from 0 to 223, as said below
- far_count: int32 [32, 16], P('row', 'col'), may hold values from 16 to 128, as said below
Outputs:
- sample: bfloat16 [524288, 64], P(('row', 'col'))
Inputs may be any that keep to these rules, and one draw needn't show every extreme that they name: `near_list`: row entries index the 64 row leaves of the device's row, column entries the 128 column leaves of its column; only the first near_count slots are used. `near_count`: used slots of one device: 64 on some device in every draw, else 64/2, /4 or /8. `far_list`: row entries index the 112 row clusters, column entries the 224 column clusters; both clusters of a slot lie on the same level; only the first far_count slots are used. `far_count`: used slots of one device: 128 on some device in every draw, else 128/2, /4 or /8.
All inputs are finite; a program needn't handle non-finite values.
Results may differ from a plain program's by a relative error of at most 0.02.
Values may be sent and summed in bfloat16 or wider, within the bound.
A program may use at most 64 MiB of HBM per device.

v0:
```python
import math

import jax
import jax.numpy as jnp
from jax import lax
from jax.sharding import PartitionSpec as P

LEAF = 256
RANK = 64
SAMPLES = 64


length_scale = 0.15
root_three = math.sqrt(3.0)


def matern(first, second):
    first = first.astype(jnp.float32)
    second = second.astype(jnp.float32)
    dist = jnp.zeros(first.shape[1:] + second.shape[-1:], jnp.float32)
    for axis in range(3):
        gap = first[axis][..., :, None] - second[axis][..., None, :]
        dist = dist + gap * gap
    scaled = root_three * jnp.sqrt(dist) / length_scale
    return (1.0 + scaled) * jnp.exp(-scaled)


def upward(probe_rows, basis_rows, move_rows):
    leaf = jnp.einsum(
        "klr,kls->krs",
        basis_rows.reshape(4, LEAF, RANK),
        probe_rows.reshape(4, LEAF, SAMPLES),
        preferred_element_type=jnp.float32,
    ).astype(jnp.bfloat16)
    moves = move_rows.reshape(6, RANK, RANK)
    middle = jnp.einsum("kap,kas->kps", moves[0:4], leaf, preferred_element_type=jnp.float32)
    middle = middle.reshape(2, 2, RANK, SAMPLES).sum(axis=1).astype(jnp.bfloat16)
    upper = jnp.einsum("kap,kas->kps", moves[4:6], middle, preferred_element_type=jnp.float32)
    upper = upper.sum(axis=0, keepdims=True).astype(jnp.bfloat16)
    return jnp.concatenate([leaf, middle, upper], axis=0)


def near_terms(row_points, col_points, col_probes, pairs, live, groups):
    row_leaves = row_points.reshape(3, -1, LEAF)
    col_leaves = col_points.reshape(3, -1, LEAF)
    col_values = col_probes.reshape(-1, LEAF, SAMPLES)
    totals = jnp.zeros((row_leaves.shape[1], LEAF, SAMPLES), jnp.float32)

    def near_step(group, totals):
        slots = lax.dynamic_slice_in_dim(pairs, group * 4, 4, 1)
        alive = group * 4 + jnp.arange(4, dtype=jnp.int32) < live
        targets = slots[0]
        sources = slots[1]
        kernel = matern(row_leaves[:, targets], col_leaves[:, sources]).astype(jnp.bfloat16)
        term = jnp.einsum(
            "gab,gbs->gas", kernel, col_values[sources], preferred_element_type=jnp.float32
        )
        term = jnp.where(alive[:, None, None], term, 0.0)
        return totals.at[targets].add(term)

    totals = lax.fori_loop(0, groups, near_step, totals)
    return totals.reshape(-1, SAMPLES)


def far_terms(row_skel, col_skel, col_coeffs, pairs, live, groups):
    row_sets = row_skel.reshape(3, -1, RANK)
    col_sets = col_skel.reshape(3, -1, RANK)
    totals = jnp.zeros((row_sets.shape[1], RANK, SAMPLES), jnp.float32)

    def far_step(group, totals):
        slots = lax.dynamic_slice_in_dim(pairs, group * 16, 16, 1)
        alive = group * 16 + jnp.arange(16, dtype=jnp.int32) < live
        targets = slots[0]
        sources = slots[1]
        kernel = matern(row_sets[:, targets], col_sets[:, sources]).astype(jnp.bfloat16)
        term = jnp.einsum(
            "gab,gbs->gas", kernel, col_coeffs[sources], preferred_element_type=jnp.float32
        )
        term = jnp.where(alive[:, None, None], term, 0.0)
        return totals.at[targets].add(term)

    return lax.fori_loop(0, groups, far_step, totals)


def descend(far_total, moves):
    moves = moves.astype(jnp.float32)
    upper = far_total[:, 6]
    middle = far_total[:, 4:6] + jnp.einsum(
        "dkab,dbs->dkas", moves[:, 4:6], upper, precision=lax.Precision.HIGHEST
    )
    spread = jnp.repeat(middle, 2, axis=1)
    return far_total[:, 0:4] + jnp.einsum(
        "dkab,dkbs->dkas", moves[:, 0:4], spread, precision=lax.Precision.HIGHEST
    )


def local(
    probes, points, skeleton, leaf_basis, transfer, near_list, near_count, far_list, far_count
):
    row_count = lax.axis_size("row")
    col_count = lax.axis_size("col")
    col_probes, col_points, col_skel, col_basis, col_moves = (
        lax.all_gather(probes, "row", axis=0, tiled=True),
        lax.all_gather(points, "row", axis=1, tiled=True),
        lax.all_gather(skeleton, "row", axis=1, tiled=True),
        lax.all_gather(leaf_basis, "row", axis=0, tiled=True),
        lax.all_gather(transfer, "row", axis=0, tiled=True),
    )
    col_coeffs = jax.vmap(upward)(
        col_probes.reshape(row_count, 4 * LEAF, SAMPLES),
        col_basis.reshape(row_count, 4 * LEAF, RANK),
        col_moves.reshape(row_count, 6 * RANK, RANK),
    )
    col_coeffs = col_coeffs.reshape(row_count * 7, RANK, SAMPLES)
    row_points, row_skel, row_moves = (
        lax.all_gather(points, "col", axis=1, tiled=True),
        lax.all_gather(skeleton, "col", axis=1, tiled=True),
        lax.all_gather(transfer, "col", axis=0, tiled=True),
    )
    near_pairs = near_list[0, 0]
    far_pairs = far_list[0, 0]
    near_live = near_count[0, 0]
    far_live = far_count[0, 0]
    near_groups = near_pairs.shape[1] // 4
    far_groups = far_pairs.shape[1] // 16
    near_part = near_terms(row_points, col_points, col_probes, near_pairs, near_live, near_groups)
    far_part = far_terms(row_skel, col_skel, col_coeffs, far_pairs, far_live, far_groups)
    near_own = lax.psum_scatter(
        near_part.astype(jnp.bfloat16), "col", scatter_dimension=0, tiled=True
    ).astype(jnp.float32)
    leaf_far = descend(
        far_part.reshape(col_count, 7, RANK, SAMPLES), row_moves.reshape(col_count, 6, RANK, RANK)
    )
    leaf_own = lax.psum_scatter(
        leaf_far.reshape(-1, SAMPLES).astype(jnp.bfloat16), "col", scatter_dimension=0, tiled=True
    ).astype(jnp.float32)
    leaf_own = leaf_own.reshape(4, RANK, SAMPLES)
    expanded = jnp.einsum(
        "klr,krs->kls",
        leaf_basis.reshape(4, LEAF, RANK).astype(jnp.float32),
        leaf_own,
        precision=lax.Precision.HIGHEST,
    )
    result = near_own.reshape(4, LEAF, SAMPLES) + expanded
    return result.reshape(4 * LEAF, SAMPLES).astype(jnp.bfloat16)


def solution(mesh):
    placed = (
        P(("row", "col"), None),
        P(None, ("row", "col")),
        P(None, ("row", "col")),
        P(("row", "col"), None),
        P(("row", "col"), None),
        P("row", "col", None, None),
        P("row", "col"),
        P("row", "col", None, None),
        P("row", "col"),
    )
    return jax.shard_map(
        local, mesh=mesh, in_specs=placed, out_specs=P(("row", "col"), None), check_vma=False
    )
```

profile of v0, /device:TPU:1, one launch (start us, length us, event | category | flops | bytes accessed | tf_op | source)
XLA Modules:
  0.0 685.8 jit_solution(6554964696894158972)
XLA Ops:
  8.8 75.3 %all-gather.1 = bf16[32,448,3]{1,2,0:T(4,128)(2,1)S(1)} all-gather(bf16[1,448,3]{1,2,0:T(4,128)(2,1)} %bitcast.207), channel_id=1, replica_groups=mesh['row'=32,'col'=16] {'row'}, dimensions={0}, use_global_device_ids=true | all-gather | bytes 88704 | tf_op jit(solution)/shard_map/all_gather | solution.py:105
  84.6 34.5 %all-gather = bf16[16,448,3]{1,2,0:T(4,128)(2,1)S(1)} all-gather(bf16[1,448,3]{1,2,0:T(4,128)(2,1)} %bitcast.208), channel_id=1, replica_groups=mesh['row'=32,'col'=16] {'col'}, dimensions={0}, use_global_device_ids=true | all-gather | bytes 45696 | tf_op jit(solution)/shard_map/all_gather | solution.py:117
  119.4 19.0 %all_gather.31 = bf16[6144,64]{0,1:T(8,128)(2,1)S(1)} all-gather(bf16[384,64]{0,1:T(8,128)(2,1)} %param.17), channel_id=1, replica_groups=mesh['row'=32,'col'=16] {'col'}, dimensions={0}, use_global_device_ids=true | all-gather | bytes 835584 | tf_op jit(solution)/shard_map/all_gather | solution.py:118
  140.0 20.4 %all_gather.24 = bf16[3,16384]{1,0:T(4,128)(2,1)} all-gather(bf16[3,1024]{1,0:T(4,128)(2,1)S(1)} %copy-done.4), channel_id=1, replica_groups=mesh['row'=32,'col'=16] {'col'}, dimensions={1}, use_global_device_ids=true | all-gather | bytes 104448 | tf_op jit(solution)/shard_map/all_gather | solution.py:116
  160.4 69.1 %all_gather.25 = bf16[3,32768]{1,0:T(4,128)(2,1)} all-gather(bf16[3,1024]{1,0:T(4,128)(2,1)S(1)} %copy-done.4), channel_id=1, replica_groups=mesh['row'=32,'col'=16] {'row'}, dimensions={1}, use_global_device_ids=true | all-gather | bytes 202752 | tf_op jit(solution)/shard_map/all_gather | solution.py:104
  229.5 3.1 copy.50
  232.6 7.9 %reshape_reshape.10 = bf16[32,4,256,64]{2,1,0,3:T(4,128)(2,1)} reshape(bf16[32768,64]{0,1:T(8,128)(2,1)} %all-gather.6.cloned.1.call-done) | data formatting | bytes 8388608 | tf_op jit(solution)/shard_map/vmap()/reshape;reshape | solution.py:32
  240.5 64.1 %all-gather.8.cloned.1.call-done = bf16[32768,64]{0,1:T(8,128)(2,1)} async-done(((bf16[1024,64]{0,1:T(8,128)(2,1)}), bf16[32768,64]{0,1:T(8,128)(2,1)}) %all-gather.8.cloned.1.call-update) | async-done | bytes 4194320 | tf_op jit(solution)/shard_map/all_gather | solution.py:106
  304.6 7.9 %reshape_reshape.9 = bf16[32,4,256,64]{2,1,0,3:T(4,128)(2,1)} reshape(bf16[32768,64]{0,1:T(8,128)(2,1)} %all-gather.8.cloned.1.call-done) | data formatting | bytes 8388608 | tf_op jit(solution)/shard_map/vmap()/reshape;reshape | solution.py:31
  312.5 8.2 %fusion.30 = bf16[32,4,64,64]{3,2,1,0:T(8,128)(2,1)S(1)} fusion(bf16[32,4,256,64]{2,1,0,3:T(4,128)(2,1)} %reshape_reshape.10, bf16[32,4,256,64]{2,1,0,3:T(4,128)(2,1)} %reshape_reshape.9), kind=kOutput, calls=%fused_computation.67 | convolution fusion | flops 268959744 | bytes 9437184 | tf_op jit(solution)/shard_map/vmap(klr,kls->krs)/dot_general | solution.py:29
  320.7 2.8 fusion.27
  323.5 4.0 reduce_sum.8
  331.7 3.2 pad_maximum_fusion
  334.9 2.3 broadcast_in_dim.99
  337.2 65.3 %while.31 = (s32[]{:T(128)}, f32[112,64,64]{2,1,0:T(8,128)}, s32[2,128]{1,0:T(2,128)S(1)}, s32[]{:T(128)}, bf16[3,112,64]{2,0,1:T(4,128)(2,1)S(1)}, /*index=5*/b...) while((s32[]{:T(128)}, f32[112,64,64]{2,1,0:T(8,128)}, ...), condition=%wide.region_7.8_spmd, body=%wide.region_5.7_spmd.sunk | while | flops 9379974 | bytes 1586247 | solution.py:82
  338.6 2.6 gather_fusion.3
  342.7 2.7 scatter_fusion.1
  346.8 2.6 gather_fusion.3
  350.9 2.7 scatter_fusion.1
  354.9 2.6 gather_fusion.3
  359.1 2.6 scatter_fusion.1
  363.1 2.6 gather_fusion.3
  367.2 2.7 scatter_fusion.1
  371.2 2.6 gather_fusion.3
  375.4 2.7 scatter_fusion.1
  379.4 2.6 gather_fusion.3
  383.6 2.7 scatter_fusion.1
  387.6 2.6 gather_fusion.3
  391.7 2.7 scatter_fusion.1
  395.7 2.6 gather_fusion.3
  399.9 2.7 scatter_fusion.1
  403.9 3.2 slice.214
  409.5 3.0 fusion.35
  417.2 8.4 %copy.44 = bf16[32768,64]{1,0:T(8,128)(2,1)} copy(bf16[32768,64]{0,1:T(8,128)(2,1)} %all-gather.6.cloned.1.call-done) | data formatting | bytes 8388608 | tf_op jit(solution)/shard_map/all_gather | solution.py:103
  425.7 2.5 broadcast_in_dim.98
  428.2 182.7 %while.30 = (s32[]{:T(128)}, f32[64,256,64]{1,2,0:T(8,128)}, s32[2,64]{1,0:T(2,128)S(1)}, s32[]{:T(128)}, bf16[3,64,256]{2,0,1:T(4,128)(2,1)}, /*index=5*/bf16[3...) while((s32[]{:T(128)}, f32[64,256,64]{1,2,0:T(8,128)}, ...), condition=%wide.region_2.3_spmd, body=%wide.region_0.2_spmd.sunk | while | flops 37101604 | bytes 1634703 | solution.py:61
  431.4 4.0 gather_fusion
  437.3 2.3 scatter_fusion
  442.8 4.0 gather_fusion
  454.2 4.0 gather_fusion
  465.6 4.0 gather_fusion
  477.1 4.0 gather_fusion
  483.0 2.3 scatter_fusion
  488.5 4.0 gather_fusion
  499.9 4.0 gather_fusion
  505.8 2.3 scatter_fusion
  511.3 4.0 gather_fusion
  517.2 2.3 scatter_fusion
  522.7 4.0 gather_fusion
  528.6 2.3 scatter_fusion
  534.1 4.0 gather_fusion
  540.0 2.3 scatter_fusion
  545.5 4.0 gather_fusion
  551.4 2.3 scatter_fusion
  557.0 4.0 gather_fusion
  568.4 4.0 gather_fusion
  574.3 2.3 scatter_fusion
  579.8 4.0 gather_fusion
  585.7 2.3 scatter_fusion
  591.2 4.0 gather_fusion
  597.1 2.3 scatter_fusion
  602.6 4.0 gather_fusion
  610.8 2.5 convert_bitcast_fusion.4
  615.7 61.8 %reduce-scatter.3.cloned.1.call-done = bf16[1024,64]{0,1:T(8,128)(2,1)} async-done(((bf16[16384,64]{0,1:T(8,128)(2,1)}), bf16[1024,64]{0,1:T(8,128)(2,1)}) %reduce-scatter.3.cloned.1.call-update) | async-done | bytes 131088 | tf_op jit(solution)/shard_map/reduce_scatter | solution.py:128
  (416 shorter events, 138.1 us)
Async XLA Ops:
  6.5 133.4 %copy-start.4 = (bf16[3,1024]{1,0:T(4,128)(2,1)S(1)}, bf16[3,1024]{1,0:T(4,128)(2,1)}, u32[]{:S(2)}) copy-start(bf16[3,1024]{1,0:T(4,128)(2,1)} %param.14) | copy-start | bytes 18436
  6.5 222.9 %all-gather.10.cloned.1.call-start = ((), (), s32[]{:S(2)}) async-start(), calls=%async_computation.5 | async-start | bytes 1622016 | tf_op jit(solution)/shard_map/all_gather | solution.py:107
  7.3 225.3 %all-gather.6.cloned.1.call-start = ((), (), s32[]{:S(2)}) async-start(), calls=%async_computation.2 | async-start | bytes 4325376 | tf_op jit(solution)/shard_map/all_gather | solution.py:103
  8.0 296.6 %all-gather.8.cloned.1.call-start = ((), (), s32[]{:S(2)}) async-start(), calls=%async_computation.4 | async-start | bytes 4325376 | tf_op jit(solution)/shard_map/all_gather | solution.py:106
  8.7 606.1 %reduce-scatter.5.cloned.1.call-start = ((), (), s32[]{:S(2)}) async-start(), calls=%async_computation.6 | async-start | bytes 557056 | tf_op jit(solution)/shard_map/reduce_scatter | solution.py:134
  320.7 2.8 copy-start
  329.8 1.9 copy-start.1
  334.9 2.3 copy-start.5
  409.5 3.3 copy-start.2
  417.2 260.4 %reduce-scatter.3.cloned.1.call-start = ((), (), s32[]{:S(2)}) async-start(), calls=%async_computation.3 | async-start | bytes 2228224 | tf_op jit(solution)/shard_map/reduce_scatter | solution.py:128
  425.7 2.5 copy-start.6
  613.3 65.1 %copy-start.3 = (bf16[1024,64]{0,1:T(8,128)(2,1)S(1)}, bf16[1024,64]{0,1:T(8,128)(2,1)}, u32[]{:S(2)}) copy-start(bf16[1024,64]{0,1:T(8,128)(2,1)} %param.16) | copy-start | bytes 393220
Sparse Core Ops, SparseCore 0:
  10.4 87.8 all-gather.9
  101.4 100.2 all-gather.5
  204.8 99.7 all-gather.7
  417.3 59.8 reduce-scatter.4
  615.0 62.5 reduce-scatter.2
where the time goes:
time: 692 us; the launch traced here: 686 us
  blocking collectives  218 us (32%)
  local copies, waits for them, and re-layouts  194 us (28%)
  waiting for transfers between devices  128 us (18%)
  other arithmetic  85.3 us (12%)
  matrix products  44.5 us (6%)
  between operations  13.3 us (2%)
    all_gather x1, blocking collectives, local(): lax.all_gather(skeleton, 'row', axis=1, tiled=True)  75.3 us
    all_gather x1, blocking collectives, local(): lax.all_gather(points, 'row', axis=1, tiled=True)  69.1 us
    all_gather x1, waiting for transfers between devices, local(): lax.all_gather(leaf_basis, 'row', axis=0, tiled=True)  64.1 us
    gather x16, local copies, waits for them, and re-layouts, near_step(): col_values[sources]  63.7 us
    reduce_scatter x1, waiting for transfers between devices, local(): lax.psum_scatter(near_part.astype(jnp.bfloat16), 'col', scatter_dimension...  61.8 us
    scatter-add x16, other arithmetic, near_step(): return totals.at[targets].add(term)  36.9 us
    all_gather x1, blocking collectives, local(): lax.all_gather(skeleton, 'col', axis=1, tiled=True)  34.5 us
    gather x16, local copies, waits for them, and re-layouts, near_step(): col_leaves[:, sources]  24.3 us
  transfers between devices with their start and end apart: 5, of which 2 were waited for; matrix products, arithmetic and copies ran while one was open for 31% of the time, Pallas kernels for 0%

commit v1 on v0

v1 whole, which is shorter than its diff:
```python
import math

import jax
import jax.numpy as jnp
import numpy as np
from jax import lax
from jax.experimental import pallas as pl
from jax.experimental.pallas import tpu as pltpu
from jax.sharding import PartitionSpec as P

LEAF = 256
RANK = 64
SAMPLES = 64
N_ROW = 32
N_COL = 16
N_Y = 8
N_ZH = 4
NEAR_MOST = 64
FAR_MOST = 128
PACK = 640
MESH = pl.DeviceIdType.MESH
F32 = jnp.float32
BF16 = jnp.bfloat16
RATE = math.sqrt(3.0) / 0.15
RATE2 = RATE * math.log2(math.e)


def dot_t(a, b):
    return lax.dot_general(a, b, (((1,), (1,)), ((), ())), preferred_element_type=F32)


def dot_l(a, b):
    return lax.dot_general(a, b, (((0,), (0,)), ((), ())), preferred_element_type=F32)


def dot_n(a, b):
    return jnp.dot(a, b, preferred_element_type=F32)


def selections():
    col = np.zeros((4, 16, 32), np.float32)
    row = np.zeros((4, 16, 32), np.float32)
    for k in range(4):
        for i in range(3):
            col[k, i, i * 4 + k] = -2.0
            row[k, i, i * 4 + k] = 1.0
            col[k, 3 + i, 16 + 4 * i + k] = 1.0
            row[k, 3 + i, 28] = 1.0
            col[k, 6 + i, 28] = 1.0
            row[k, 6 + i, 16 + 4 * i + k] = 1.0
    return np.concatenate([col.reshape(64, 32), row.reshape(64, 32)], axis=0)


def coordinates(points, skeleton):
    pts = points.reshape(12, LEAF)
    skel = jnp.pad(skeleton, ((0, 0), (0, 64))).reshape(12, 128)
    zero = jnp.zeros((4, 128), BF16)
    return jnp.concatenate(
        [pts[:, :128], zero, pts[:, 128:], zero, skel, zero, jnp.zeros((16, 128), BF16)], axis=0
    )


def upward_packet(probes_t, basis_t, moves_t):
    leaves = [
        dot_t(probes_t[:, k * LEAF : (k + 1) * LEAF], basis_t[:, k * LEAF : (k + 1) * LEAF])
        for k in range(4)
    ]
    leaf = jnp.concatenate(leaves, axis=1).astype(BF16)
    mids = [
        dot_t(leaf[:, j * 128 : (j + 1) * 128], moves_t[:, j * 128 : (j + 1) * 128])
        for j in range(2)
    ]
    mid = jnp.concatenate(mids, axis=1).astype(BF16)
    top = dot_t(mid, moves_t[:, 256:384]).astype(BF16)
    return jnp.concatenate([leaf, mid, top, jnp.zeros((64, 64), BF16)], axis=1)


def gather_kernel(
    probes_any, probes_t, basis_t, moves_t, geo, all_p, all_q, all_g,
    pack, send, recv_p, recv_q, recv_g, local_sem,
):
    r = lax.axis_index("row")
    c = lax.axis_index("col")
    zh = r // N_Y
    y = r % N_Y
    up = ((zh + 1) % N_ZH) * N_Y + y
    down = ((zh + 3) % N_ZH) * N_Y + y
    right = zh * N_Y + (y + 1) % N_Y
    left = zh * N_Y + (y + 7) % N_Y

    def slot(dz, dy):
        return ((zh + dz) % N_ZH) * N_Y + (y + dy) % N_Y

    barrier = pltpu.get_barrier_semaphore()
    for row in (up, down, right, left):
        pl.semaphore_signal(barrier, inc=1, device_id=(row, c), device_id_type=MESH)

    @pl.loop(1, N_COL)
    def _(d):
        pl.semaphore_signal(
            barrier, inc=1, device_id=(r, (c + d) % N_COL), device_id_type=MESH
        )

    pack[:, 0:512] = upward_packet(probes_t[...], basis_t[...], moves_t[...])
    pack[:, 512:640] = geo[...]
    pl.semaphore_wait(barrier, 4 + N_COL - 1)

    sends = []

    def copy(src, dst, sem, row):
        one = pltpu.make_async_remote_copy(
            src_ref=src, dst_ref=dst, send_sem=send.at[len(sends)], recv_sem=sem,
            device_id=(row, c), device_id_type=MESH,
        )
        one.start()
        sends.append(one)

    def arrived(dst, sem):
        pltpu.make_async_remote_copy(
            src_ref=dst, dst_ref=dst, send_sem=send.at[0], recv_sem=sem,
            device_id=(r, c), device_id_type=MESH,
        ).wait_recv()

    halves = (pl.ds(0, 32), pl.ds(32, 32))

    def mover(buf, sems):
        def push(s, row, src=None):
            copy(buf.at[s] if src is None else src, buf.at[s], sems.at[s, 0], row)

        def push_half(s, h, row):
            copy(buf.at[s, halves[h]], buf.at[s, halves[h]], sems.at[s, h], row)

        def wait(s):
            arrived(buf.at[s], sems.at[s, 0])

        def wait_half(s, h):
            arrived(buf.at[s, halves[h]], sems.at[s, h])

        return push, push_half, wait, wait_half

    p_push, p_push_half, p_wait, p_wait_half = mover(all_p, recv_p)
    q_push, q_push_half, q_wait, q_wait_half = mover(all_q, recv_q)
    me = slot(0, 0)

    q_push(me, right, pack)
    q_push(me, left, pack)
    p_push(me, up, probes_any)
    p_push(me, down, probes_any)
    p_push(me, right, probes_any)
    p_push(me, left, probes_any)
    q_push(me, up, pack)
    q_push(me, down, pack)

    @pl.loop(1, N_COL)
    def _(d):
        pltpu.make_async_remote_copy(
            src_ref=pack.at[:, pl.ds(512, 128)], dst_ref=all_g.at[c],
            send_sem=recv_g.at[0, d], recv_sem=recv_g.at[1, d],
            device_id=(r, (c + d) % N_COL), device_id_type=MESH,
        ).start()

    own = [
        pltpu.make_async_copy(probes_any, all_p.at[me], local_sem.at[0]),
        pltpu.make_async_copy(pack, all_q.at[me], local_sem.at[1]),
        pltpu.make_async_copy(pack.at[:, pl.ds(512, 128)], all_g.at[c], local_sem.at[2]),
    ]
    for one in own:
        one.start()

    p_wait(slot(3, 0))
    p_push_half(slot(3, 0), 0, up)
    p_wait(slot(1, 0))
    p_push_half(slot(1, 0), 1, down)
    for dz in (3, 1):
        p_push(slot(dz, 0), right)
        p_push(slot(dz, 0), left)
    p_wait_half(slot(2, 0), 0)
    p_wait_half(slot(2, 0), 1)
    p_push(slot(2, 0), right)
    p_push(slot(2, 0), left)

    def q_z_forward(dy):
        q_wait(slot(3, dy))
        q_push_half(slot(3, dy), 0, up)
        q_wait(slot(1, dy))
        q_push_half(slot(1, dy), 1, down)

    q_z_forward(0)
    for k in (1, 2, 3):
        q_wait(slot(0, -k))
        if k < 3:
            q_push(slot(0, -k), right)
        else:
            q_push_half(slot(0, -k), 0, right)
        q_wait(slot(0, k))
        if k < 3:
            q_push(slot(0, k), left)
        else:
            q_push_half(slot(0, k), 1, left)
        for dy in (-k, k):
            q_push(slot(0, dy), up)
            q_push(slot(0, dy), down)
        for dz in (0, 3, 1, 2):
            p_wait(slot(dz, -k))
            if k < 3:
                p_push(slot(dz, -k), right)
            else:
                p_push_half(slot(dz, -k), 0, right)
            p_wait(slot(dz, k))
            if k < 3:
                p_push(slot(dz, k), left)
            else:
                p_push_half(slot(dz, k), 1, left)
        if k == 3:
            q_wait_half(slot(0, 4), 0)
            q_wait_half(slot(0, 4), 1)
            q_push(slot(0, 4), up)
            q_push(slot(0, 4), down)
        for dy in (-k, k):
            q_z_forward(dy)
    q_z_forward(4)
    for dz in (0, 3, 1, 2):
        p_wait_half(slot(dz, 4), 0)
        p_wait_half(slot(dz, 4), 1)
    for dy in (0, -1, 1, -2, 2, -3, 3, 4):
        q_wait_half(slot(2, dy), 0)
        q_wait_half(slot(2, dy), 1)

    @pl.loop(1, N_COL)
    def _(d):
        pltpu.make_async_remote_copy(
            src_ref=pack.at[:, pl.ds(512, 128)], dst_ref=all_g.at[(c + N_COL - d) % N_COL],
            send_sem=recv_g.at[0, d], recv_sem=recv_g.at[1, d],
            device_id=(r, (c + d) % N_COL), device_id_type=MESH,
        ).wait()

    for one in own:
        one.wait()
    for one in sends:
        one.wait_send()


def gather(probes_t, basis_t, moves_t, geo):
    vmem = pl.BlockSpec(memory_space=pltpu.VMEM)
    anywhere = pl.BlockSpec(memory_space=pl.ANY)
    return pl.pallas_call(
        gather_kernel,
        out_shape=(
            jax.ShapeDtypeStruct((N_ROW, 64, 1024), BF16),
            jax.ShapeDtypeStruct((N_ROW, 64, PACK), BF16),
            jax.ShapeDtypeStruct((N_COL, 64, 128), BF16),
        ),
        in_specs=[anywhere, vmem, vmem, vmem, vmem],
        out_specs=(anywhere, anywhere, anywhere),
        scratch_shapes=[
            pltpu.VMEM((64, PACK), BF16),
            pltpu.SemaphoreType.DMA((80,)),
            pltpu.SemaphoreType.DMA((N_ROW, 2)),
            pltpu.SemaphoreType.DMA((N_ROW, 2)),
            pltpu.SemaphoreType.DMA((2, N_COL)),
            pltpu.SemaphoreType.DMA((3,)),
        ],
        compiler_params=pltpu.CompilerParams(
            collective_id=0, has_side_effects=True, vmem_limit_bytes=32 << 20
        ),
        name="gather",
    )(probes_t, probes_t, basis_t, moves_t, geo)


def features(sel, geo):
    flat = jnp.concatenate([geo[0:16], geo[16:32], geo[32:48]], axis=1).astype(F32)
    squares = flat * flat
    norm = squares[0:4] + squares[4:8] + squares[8:12]
    high = norm.astype(BF16).astype(F32)
    rest = norm - high
    middle = rest.astype(BF16).astype(F32)
    low = rest - middle
    stack = jnp.concatenate([flat, high, middle, low, jnp.ones_like(norm)], axis=0)
    return dot_n(sel, stack.astype(BF16)).astype(BF16)


def matern(square):
    square = jnp.maximum(square, 1e-30)
    dist = square * lax.rsqrt(square)
    return ((1.0 + RATE * dist) * jnp.exp2(dist * (-RATE2))).astype(BF16)


def blocks_kernel(
    near_list, near_count, far_list, far_count, sel, all_p, all_q, all_g, near_out, far_out,
    col_leaf, row_leaf, col_skel, row_skel, coeffs, near_acc, far_acc,
):
    @pl.loop(0, N_ROW)
    def _(d):
        feat = features(sel[0:64], all_q[d, :, 512:640])
        col_leaf[pl.ds(d * 4, 4)] = feat[:, 0:256].reshape(4, 16, 256)
        for j in range(7):
            half = feat[(j // 2) * 16 : (j // 2) * 16 + 16, 256 + (j % 2) * 64 : 320 + (j % 2) * 64]
            col_skel[d * 7 + j] = half
            coeffs[d * 7 + j] = all_q[d, :, j * 64 : (j + 1) * 64]

    @pl.loop(0, N_COL)
    def _(d):
        feat = features(sel[64:128], all_g[d])
        row_leaf[pl.ds(d * 4, 4)] = feat[:, 0:256].reshape(4, 16, 256)
        for j in range(7):
            half = feat[(j // 2) * 16 : (j // 2) * 16 + 16, 256 + (j % 2) * 64 : 320 + (j % 2) * 64]
            row_skel[d * 7 + j] = half

    near_acc[...] = jnp.zeros_like(near_acc)
    far_acc[...] = jnp.zeros_like(far_acc)

    @pl.loop(0, near_count[0, 0] // 2)
    def _(g):
        for u in range(2):
            a = near_list[0, g * 2 + u]
            b = near_list[1, g * 2 + u]
            kern = matern(dot_l(col_leaf[b], row_leaf[a]))
            lanes = pl.ds(pl.multiple_of((b % 4) * LEAF, LEAF), LEAF)
            near_acc[a] += dot_n(all_p[b // 4, :, lanes], kern)

    @pl.loop(0, far_count[0, 0] // 8)
    def _(g):
        for u in range(8):
            a = far_list[0, g * 8 + u]
            b = far_list[1, g * 8 + u]
            kern = matern(dot_l(col_skel[b], row_skel[a]))
            far_acc[a] += dot_n(coeffs[b], kern)

    @pl.loop(0, N_COL)
    def _(d):
        for k in range(4):
            near_out[d, :, k * LEAF : (k + 1) * LEAF] = near_acc[d * 4 + k].astype(BF16)
        for j in range(4):
            low = far_acc[d * 7 + 2 * j]
            high = far_acc[d * 7 + 2 * j + 1] if j < 3 else jnp.zeros((64, 64), F32)
            far_out[d, :, j * 128 : (j + 1) * 128] = jnp.concatenate([low, high], axis=1).astype(BF16)


def blocks(near_list, near_count, far_list, far_count, sel, all_p, all_q, all_g):
    vmem = pl.BlockSpec(memory_space=pltpu.VMEM)
    smem = pl.BlockSpec(memory_space=pltpu.SMEM)
    return pl.pallas_call(
        blocks_kernel,
        out_shape=(
            jax.ShapeDtypeStruct((N_COL, 64, 1024), BF16),
            jax.ShapeDtypeStruct((N_COL, 64, 512), BF16),
        ),
        in_specs=[smem, smem, smem, smem, vmem, vmem, vmem, vmem],
        out_specs=(vmem, vmem),
        scratch_shapes=[
            pltpu.VMEM((4 * N_ROW, 16, LEAF), BF16),
            pltpu.VMEM((4 * N_COL, 16, LEAF), BF16),
            pltpu.VMEM((7 * N_ROW, 16, RANK), BF16),
            pltpu.VMEM((7 * N_COL, 16, RANK), BF16),
            pltpu.VMEM((7 * N_ROW, SAMPLES, RANK), BF16),
            pltpu.VMEM((4 * N_COL, SAMPLES, LEAF), F32),
            pltpu.VMEM((7 * N_COL, SAMPLES, RANK), F32),
        ],
        compiler_params=pltpu.CompilerParams(vmem_limit_bytes=48 << 20),
        name="blocks",
    )(near_list, near_count, far_list, far_count, sel, all_p, all_q, all_g)


def split_dot(a, b):
    high = a.astype(BF16)
    low = (a - high.astype(F32)).astype(BF16)
    both = dot_n(jnp.concatenate([high, low], axis=0), b)
    return both[: a.shape[0]] + both[a.shape[0] :]


def reduce_kernel(
    near, far, basis_t, moves_t, out,
    near_sib, far_sib, near_sum, far_sum, near_in, far_in, sems, sib_sems,
):
    r = lax.axis_index("row")
    c = lax.axis_index("col")
    core = c % 2
    chip = c // 2
    sibling = chip * 2 + 1 - core

    barrier = pltpu.get_barrier_semaphore()
    pl.semaphore_signal(barrier, inc=1, device_id=(r, sibling), device_id_type=MESH)

    @pl.loop(1, 8)
    def _(d):
        other = ((chip + d) % 8) * 2 + core
        pl.semaphore_signal(barrier, inc=1, device_id=(r, other), device_id_type=MESH)

    pl.semaphore_wait(barrier, 8)

    def sib_copy(d, src_chip):
        theirs = src_chip * 2 + 1 - core
        return (
            pltpu.make_async_remote_copy(
                src_ref=near.at[theirs], dst_ref=near_sib.at[d],
                send_sem=sib_sems.at[0, d], recv_sem=sib_sems.at[1, d],
                device_id=(r, sibling), device_id_type=MESH,
            ),
            pltpu.make_async_remote_copy(
                src_ref=far.at[theirs], dst_ref=far_sib.at[d],
                send_sem=sib_sems.at[2, d], recv_sem=sib_sems.at[3, d],
                device_id=(r, sibling), device_id_type=MESH,
            ),
        )

    def chip_copy(d):
        other = ((chip + d) % 8) * 2 + core
        return (
            pltpu.make_async_remote_copy(
                src_ref=near_sum.at[d], dst_ref=near_in.at[d],
                send_sem=sems.at[0, d], recv_sem=sems.at[1, d],
                device_id=(r, other), device_id_type=MESH,
            ),
            pltpu.make_async_remote_copy(
                src_ref=far_sum.at[d], dst_ref=far_in.at[d],
                send_sem=sems.at[2, d], recv_sem=sems.at[3, d],
                device_id=(r, other), device_id_type=MESH,
            ),
        )

    @pl.loop(0, 8)
    def _(i):
        d = 7 - i
        for one in sib_copy(d, (chip + d) % 8):
            one.start()

    @pl.loop(0, 7)
    def _(i):
        d = 7 - i
        for one in sib_copy(d, (chip + d) % 8):
            one.wait_recv()
        mine = ((chip + d) % 8) * 2 + core
        near_sum[d] = (near[mine].astype(F32) + near_sib[d].astype(F32)).astype(BF16)
        far_sum[d] = (far[mine].astype(F32) + far_sib[d].astype(F32)).astype(BF16)
        for one in chip_copy(d):
            one.start()

    for one in sib_copy(0, chip):
        one.wait_recv()
    near_total = near[c].astype(F32) + near_sib[0].astype(F32)
    far_total = far[c].astype(F32) + far_sib[0].astype(F32)
    near_keep = near_total
    for d in range(1, 8):
        for one in chip_copy(d):
            one.wait_recv()
        near_keep = near_keep + near_in[d].astype(F32)
        far_total = far_total + far_in[d].astype(F32)

    top = far_total[:, 384:448]
    middle = far_total[:, 256:384] + split_dot(top, moves_t[:, 256:384])
    for k in range(4):
        leaf = far_total[:, k * 64 : (k + 1) * 64] + split_dot(
            middle[:, (k // 2) * 64 : (k // 2) * 64 + 64], moves_t[:, k * 64 : (k + 1) * 64]
        )
        lanes = slice(k * LEAF, (k + 1) * LEAF)
        out[:, lanes] = (near_keep[:, lanes] + split_dot(leaf, basis_t[:, lanes])).astype(BF16)

    @pl.loop(0, 8)
    def _(d):
        for one in sib_copy(d, (chip + d) % 8):
            one.wait_send()

    @pl.loop(1, 8)
    def _(d):
        for one in chip_copy(d):
            one.wait_send()


def reduce(near, far, basis_t, moves_t):
    vmem = pl.BlockSpec(memory_space=pltpu.VMEM)
    return pl.pallas_call(
        reduce_kernel,
        out_shape=jax.ShapeDtypeStruct((64, 1024), BF16),
        in_specs=[vmem, vmem, vmem, vmem],
        out_specs=vmem,
        scratch_shapes=[
            pltpu.VMEM((8, 64, 1024), BF16),
            pltpu.VMEM((8, 64, 512), BF16),
            pltpu.VMEM((8, 64, 1024), BF16),
            pltpu.VMEM((8, 64, 512), BF16),
            pltpu.VMEM((8, 64, 1024), BF16),
            pltpu.VMEM((8, 64, 512), BF16),
            pltpu.SemaphoreType.DMA((4, 8)),
            pltpu.SemaphoreType.DMA((4, 8)),
        ],
        compiler_params=pltpu.CompilerParams(
            collective_id=1, has_side_effects=True, vmem_limit_bytes=32 << 20
        ),
        name="reduce",
    )(near, far, basis_t, moves_t)


def local(
    probes, points, skeleton, leaf_basis, transfer, near_list, near_count, far_list, far_count
):
    probes_t, basis_t, moves_t = probes.T, leaf_basis.T, transfer.T
    sel = jnp.asarray(selections(), BF16)
    geo = coordinates(points, skeleton)
    all_p, all_q, all_g = gather(probes_t, basis_t, moves_t, geo)
    near, far = blocks(
        near_list[0, 0], near_count, far_list[0, 0], far_count, sel, all_p, all_q, all_g
    )
    return reduce(near, far, basis_t, moves_t).T


def solution(mesh):
    placed = (
        P(("row", "col"), None),
        P(None, ("row", "col")),
        P(None, ("row", "col")),
        P(("row", "col"), None),
        P(("row", "col"), None),
        P("row", "col", None, None),
        P("row", "col"),
        P("row", "col", None, None),
        P("row", "col"),
    )
    return jax.shard_map(
        local, mesh=mesh, in_specs=placed, out_specs=P(("row", "col"), None), check_vma=False
    )
```

time: 692 us -> 154 us (0.22)
  blocking collectives: 218 us -> 0 us
  local copies, waits for them, and re-layouts: 194 us -> 8.91 us
  Pallas kernels: 0 us -> 143 us
  waiting for transfers between devices: 128 us -> 0 us
  other arithmetic: 85.3 us -> 0 us
  matrix products: 44.5 us -> 0 us
  between operations: 13.3 us -> 1.38 us
    all_gather x5 -> x0, blocking collectives: 218 us -> none  [the longest x1 75.3 us: local(): lax.all_gather(skeleton, 'row', axis=1, tiled=True)]
    pallas_call x0 -> x3, Pallas kernels: none -> 143 us  [the longest x1 73.7 us: gather(): pl.pallas_call(gather_kernel, out_shape=(jax.ShapeDtypeStruct((N_ROW, 64,...]
    gather x72 -> x0, local copies, waits for them, and re-layouts: 142 us -> none  [the longest x16 63.7 us: near_step(): col_values[sources]]
    all_gather x3 -> x0, waiting for transfers between devices: 64.2 us -> none  [the longest x1 64.1 us: local(): lax.all_gather(leaf_basis, 'row', axis=0, tiled=True)]
    reduce_scatter x2 -> x0, waiting for transfers between devices: 61.8 us -> none  [the longest x1 61.8 us: local(): lax.psum_scatter(near_part.astype(jnp.bfloat16), 'col', scatter_dimension...]
    scatter-add x24 -> x0, other arithmetic: 58.3 us -> none  [the longest x16 36.9 us: near_step(): return totals.at[targets].add(term)]
    dot_general x30 -> x0, matrix products: 44.5 us -> none  [the longest x16 19.9 us: near_step(): jnp.einsum('gab,gbs->gas', kernel, col_values[sources], preferred_element...]
    another operation x2 -> x0, local copies, waits for them, and re-layouts: 15.8 us -> none  [the longest x1 7.9 us: upward(): basis_rows.reshape(4, LEAF, RANK)]
  transfers between devices with their start and end apart: 5 -> 0, of which waited for: 2 -> 0; matrix products, arithmetic and copies ran while one was open for 31% -> 0% of each run, Pallas kernels for 0% -> 0%
where the time goes in v1:
time: 154 us; the launch traced here: 153 us
  Pallas kernels  143 us (93%)
  local copies, waits for them, and re-layouts  8.91 us (6%)
    pallas_call x1, Pallas kernels, gather(): pl.pallas_call(gather_kernel, out_shape=(jax.ShapeDtypeStruct((N_ROW, 64,...  73.7 us
    pallas_call x1, Pallas kernels, reduce(): pl.pallas_call(reduce_kernel, out_shape=jax.ShapeDtypeStruct((64, 1024),...  50.7 us
    pallas_call x1, Pallas kernels, blocks(): pl.pallas_call(blocks_kernel, out_shape=(jax.ShapeDtypeStruct((N_COL, 64,...  18.2 us
    unnamed x19, local copies, waits for them, and re-layouts  7.33 us

profile of v1, /device:TPU:1, one launch (start us, length us, event | category | flops | bytes accessed | tf_op | source)
XLA Modules:
  0.0 152.9 jit_solution(2875966465625481747)
XLA Ops:
  1.3 0.7 pad.4
  2.0 0.7 reshape.6
  2.8 0.1 concatenate.3.geo
  2.9 0.0 copy-start.1
  2.9 0.9 copy-done.1
  3.8 0.0 copy-start.2
  3.8 0.9 copy-done.2
  4.7 0.0 copy-start.4
  4.7 0.8 copy-done.4
  5.5 73.7 %gather.1 = (bf16[32,64,1024]{2,1,0:T(8,128)(2,1)S(1)}, bf16[32,64,640]{2,1,0:T(8,128)(2,1)S(1)}, bf16[16,64,128]{2,1,0:T(8,128)(2,1)S(1)}) custom-call(bf16[64,1024]{1,0:T(8,128)(2,1)S(1)} %bitcast.6, bf16[64,1024]{1,0:T(8,128)(2,1)S(1)} %bitcast.7, bf16[64,1024]{1,0:T(8,128)(2,1)S(1)} %bitcast.8, bf16[64,384]{1,0:T(8,128)(2,1)S(1)} %bitcast.11, ...), custom_call_target="tpu_custom_call" | custom-call | tf_op jit(solution)/shard_map/gather/pallas_call | solution.py:246
  79.2 0.0 copy-start
  79.2 1.9 %copy-done = bf16[32,64,1024]{2,1,0:T(8,128)(2,1)} copy-done((bf16[32,64,1024]{2,1,0:T(8,128)(2,1)}, bf16[32,64,1024]{2,1,0:T(8,128)(2,1)S(1)}, u32[]{:S(2)}) %copy-start) | copy-done | bytes 4194328
  81.2 0.0 copy-start.6
  81.2 0.8 copy-done.6
  81.9 0.0 copy-start.7
  81.9 0.7 copy-done.7
  82.6 0.0 copy-start.8
  82.6 0.7 copy-done.8
  83.3 0.0 copy-start.3
  83.3 0.0 copy-start.5
  83.3 18.2 %blocks.1 = (bf16[16,64,1024]{2,1,0:T(8,128)(2,1)S(1)}, bf16[16,64,512]{2,1,0:T(8,128)(2,1)S(1)}) custom-call(s32[2,64]{1,0:T(2,128)S(1)} %bitcast.13, s32[1,1]{1,0:T(1,128)S(6)} %copy.12.near_count, s32[2,128]{1,0:T(2,128)S(1)} %bitcast.14, s32[1,1]{1,0:T(1,128)S(6)} %copy.13.far_count, bf16[128,32]{1,0:T(8,128)(2,1)S(1)} %copy-done.6, ...), custom_call_target="tpu_custom_call" | custom-call | tf_op jit(solution)/shard_map/blocks/pallas_call | solution.py:342
  101.5 0.0 copy-done.3
  101.5 0.0 copy-done.5
  101.5 50.7 %reduce.1 = bf16[64,1024]{1,0:T(8,128)(2,1)S(1)} custom-call(bf16[16,64,1024]{2,1,0:T(8,128)(2,1)S(1)} %get-tuple-element.13.near, bf16[16,64,512]{2,1,0:T(8,128)(2,1)S(1)} %get-tuple-element.14.far, bf16[64,1024]{1,0:T(8,128)(2,1)S(1)} %bitcast.9, bf16[64,384]{1,0:T(8,128)(2,1)S(1)} %bitcast.12), custom_call_target="tpu_custom_call" | custom-call | tf_op jit(solution)/shard_map/reduce/pallas_call | solution.py:471
  152.3 0.7 copy.14
  (4 shorter events, 0.0 us)
Async XLA Ops:
  2.9 0.9 copy-start.1
  3.8 0.9 copy-start.2
  4.7 0.8 copy-start.4
  79.2 2.0 %copy-start = (bf16[32,64,1024]{2,1,0:T(8,128)(2,1)}, bf16[32,64,1024]{2,1,0:T(8,128)(2,1)S(1)}, u32[]{:S(2)}) copy-start(bf16[32,64,1024]{2,1,0:T(8,128)(2,1)S(1)} %get-tuple-element.10.all_p) | copy-start | bytes 12582916
  81.2 0.8 copy-start.6
  81.9 0.7 copy-start.7
  82.6 0.7 copy-start.8
  83.3 18.2 %copy-start.3 = (bf16[1024,64]{0,1:T(8,128)(2,1)S(1)}, bf16[1024,64]{0,1:T(8,128)(2,1)}, u32[]{:S(2)}) copy-start(bf16[1024,64]{0,1:T(8,128)(2,1)} %param.13) | copy-start | bytes 393220
  83.3 18.3 %copy-start.5 = (bf16[384,64]{0,1:T(8,128)(2,1)S(1)}, bf16[384,64]{0,1:T(8,128)(2,1)}, u32[]{:S(2)}) copy-start(bf16[384,64]{0,1:T(8,128)(2,1)} %param.14) | copy-start | bytes 147460

commit v2 on v0

v2 whole, which is shorter than its diff:
```python
import functools
import math

import jax
import jax.numpy as jnp
import numpy as np
from jax import lax
from jax.experimental import pallas as pl
from jax.experimental.pallas import tpu as pltpu
from jax.sharding import PartitionSpec as P

LEAF = 256
RANK = 64
SAMPLES = 64
N_ROW = 32
N_COL = 16
N_Y = 8
N_ZH = 4
NEAR_MOST = 64
FAR_MOST = 128
GEO = 384
MESH = pl.DeviceIdType.MESH
F32 = jnp.float32
BF16 = jnp.bfloat16
RATE = math.sqrt(3.0) / 0.15
RATE2 = RATE * math.log2(math.e)


def dot_t(a, b):
    return lax.dot_general(a, b, (((1,), (1,)), ((), ())), preferred_element_type=F32)


def dot_l(a, b):
    return lax.dot_general(a, b, (((0,), (0,)), ((), ())), preferred_element_type=F32)


def dot_n(a, b):
    return jnp.dot(a, b, preferred_element_type=F32)


def selections():
    col = np.zeros((4, 16, 32), np.float32)
    row = np.zeros((4, 16, 32), np.float32)
    for k in range(4):
        for i in range(3):
            col[k, i, i * 4 + k] = -2.0
            row[k, i, i * 4 + k] = 1.0
            col[k, 3 + i, 16 + 4 * i + k] = 1.0
            row[k, 3 + i, 28] = 1.0
            col[k, 6 + i, 28] = 1.0
            row[k, 6 + i, 16 + 4 * i + k] = 1.0
    return np.concatenate([col.reshape(64, 32), row.reshape(64, 32)], axis=0)


def upward_packet(probes_t, basis_t, moves_t):
    leaves = [
        dot_t(probes_t[:, k * LEAF : (k + 1) * LEAF], basis_t[:, k * LEAF : (k + 1) * LEAF])
        for k in range(4)
    ]
    leaf = jnp.concatenate(leaves, axis=1).astype(BF16)
    mids = [
        dot_t(leaf[:, j * 128 : (j + 1) * 128], moves_t[:, j * 128 : (j + 1) * 128])
        for j in range(2)
    ]
    mid = jnp.concatenate(mids, axis=1).astype(BF16)
    top = dot_t(mid, moves_t[:, 256:384]).astype(BF16)
    halves = jnp.concatenate([top[:32], top[32:]], axis=1)
    halves = jnp.concatenate([halves, halves], axis=0)
    return jnp.concatenate([leaf, mid, halves], axis=1)


def matern(square):
    square = jnp.maximum(square, 1e-30)
    dist = square * lax.rsqrt(square)
    return (1.0 + RATE * dist) * jnp.exp2(dist * (-RATE2))


def split_dot(a, b):
    high = a.astype(BF16)
    low = (a - high.astype(F32)).astype(BF16)
    both = dot_n(jnp.concatenate([high, low], axis=0), b)
    return both[: a.shape[0]] + both[a.shape[0] :]


def features(sel, geo):
    flat = geo.astype(F32)
    squares = flat * flat
    norm = squares[0:4] + squares[4:8] + squares[8:12]
    high = norm.astype(BF16).astype(F32)
    rest = norm - high
    middle = rest.astype(BF16).astype(F32)
    low = rest - middle
    stack = jnp.concatenate([flat, high, middle, low, jnp.ones_like(norm)], axis=0)
    return dot_n(sel, stack.astype(BF16)).astype(BF16)


def prepare_kernel(
    near_list, near_count, far_list, far_count, points, skeleton,
    geo, near_pair, near_prev, near_last, far_prev, far_last, far_pair, far_side,
):
    pts = points[...].astype(F32)
    skel = skeleton[...].astype(F32)
    rows = []
    for i in range(3):
        for k in range(4):
            tail = skel[i : i + 1, k * 128 : min(k * 128 + 128, 448)]
            if k == 3:
                tail = jnp.concatenate([tail, jnp.zeros((1, 64), F32)], axis=1)
            rows.append(jnp.concatenate([pts[i : i + 1, k * LEAF : (k + 1) * LEAF], tail], axis=1))
    rows.append(jnp.zeros((4, GEO), F32))
    geo[...] = jnp.concatenate(rows, axis=0).astype(BF16)

    @pl.loop(0, FAR_MOST)
    def _(i):
        far_last[i] = 0
        far_prev[i] = 0
        for j in range(2):
            far_pair[j, i] = 0
            far_side[2 * j, i] = 0.0
            far_side[2 * j + 1, i] = 0.0

    @pl.loop(0, NEAR_MOST)
    def _(i):
        near_last[i] = 0
        near_prev[i] = 0
        for j in range(2):
            near_pair[j, i] = 0

    @pl.loop(0, near_count[0, 0] // 8)
    def _(g):
        for u in range(8):
            s = g * 8 + u
            a = near_list[0, s]
            near_pair[0, s] = a
            near_pair[1, s] = near_list[1, s]
            near_prev[s] = near_last[a]
            near_last[a] = s + 1

    @pl.loop(0, far_count[0, 0] // 8)
    def _(g):
        for u in range(8):
            s = g * 8 + u
            a = far_list[0, s]
            far_prev[s] = far_last[a]
            far_last[a] = s + 1
            for side in range(2):
                cluster = far_list[side, s]
                device = cluster // 7
                local = cluster - device * 7
                odd = (local % 2).astype(F32)
                far_pair[side, s] = device * 4 + local // 2
                far_side[2 * side, s] = 1.0 - odd
                far_side[2 * side + 1, s] = odd


def prepare(near_list, near_count, far_list, far_count, points, skeleton):
    vmem = pl.BlockSpec(memory_space=pltpu.VMEM)
    smem = pl.BlockSpec(memory_space=pltpu.SMEM)
    ints = lambda *shape: jax.ShapeDtypeStruct(shape, jnp.int32)
    return pl.pallas_call(
        prepare_kernel,
        out_shape=(
            jax.ShapeDtypeStruct((16, GEO), BF16),
            ints(2, NEAR_MOST), ints(NEAR_MOST), ints(NEAR_MOST), ints(FAR_MOST), ints(FAR_MOST), ints(2, FAR_MOST),
            jax.ShapeDtypeStruct((4, FAR_MOST), F32),
        ),
        in_specs=[smem, smem, smem, smem, vmem, vmem],
        out_specs=(vmem,) + (smem,) * 7,
        name="prepare",
    )(near_list, near_count, far_list, far_count, points, skeleton)


ORDER = (
    "g0", "b0", "a0", "up", "gz", "q0", "a10", "gy1", "by1", "q10", "gy2", "qz1", "gy3", "by2", "q13", "gy4",
    "qz2", "az1", "q11", "by3", "bz0", "gr", "F0", "q20", "q12", "a11", "F1", "bz1", "q21", "N2", "N7", "q23",
    "N1", "az2", "q22", "by4", "q30", "a13", "K2", "N0", "N3", "K0", "q33", "K3", "q31", "N4", "q32", "q40",
    "bz3", "a12", "a21", "K1", "q43", "N5", "q42", "a23", "bz2", "q41", "N6", "bz4", "a20", "a22", "U", "M0",
    "a31", "M1", "a33", "M2", "a30", "M3", "a32", "fs", "a43", "a41", "be", "fp", "a42", "a40", "nm", "rs", "end",
)


def main_kernel(
    order,
    near_pair, near_prev, near_last, far_prev, far_last, far_pair, far_side,
    sel, probes_t, basis_t, moves_t, geo,
    out,
    all_p, all_q, col_geo, row_geo, col_leaf, row_leaf, col_skel, row_skel,
    near_k, far_k, near_c, far_c, near_out, far_out,
    near_sib, far_sib, near_sum, far_sum, near_in, far_in,
    send, recv_a, recv_b, recv_q, geo_send, geo_recv, row_sems, ring_send, ring_recv, sems, sib_sems,
):
    r = lax.axis_index("row")
    c = lax.axis_index("col")
    zh = r // N_Y
    y = r % N_Y
    core = c % 2
    chip = c // 2
    sibling = chip * 2 + 1 - core

    def slot(dz, dy):
        return ((zh + dz) % N_ZH) * N_Y + (y + dy) % N_Y

    up, down, across = slot(1, 0), slot(3, 0), slot(2, 0)
    right, left = slot(0, 1), slot(0, -1)
    me = slot(0, 0)

    barrier = pltpu.get_barrier_semaphore()
    for row in (up, down, across, right, left):
        pl.semaphore_signal(barrier, inc=1, device_id=(row, c), device_id_type=MESH)

    @pl.loop(1, N_COL)
    def _(d):
        pl.semaphore_signal(
            barrier, inc=1, device_id=(r, (c + d) % N_COL), device_id_type=MESH
        )

    col_geo[y, zh] = geo[...]
    row_geo[c] = geo[...]
    for k in range(4):
        all_p[me * 4 + k] = probes_t[:, k * LEAF : (k + 1) * LEAF]
    pl.semaphore_wait(barrier, 5 + N_COL - 1)

    sends = []
    unsent = []

    def send_later(first, last, copy_of):
        def waits():
            @pl.loop(first, last)
            def _(d):
                copy_of(d).wait_send()

        unsent.append(waits)

    def copy(src, dst, sem, row):
        one = pltpu.make_async_remote_copy(
            src_ref=src, dst_ref=dst, send_sem=send.at[len(sends)], recv_sem=sem,
            device_id=(row, c), device_id_type=MESH,
        )
        one.start()
        sends.append(one)

    def arrived(dst, sem):
        pltpu.make_async_remote_copy(
            src_ref=dst, dst_ref=dst, send_sem=send.at[0], recv_sem=sem,
            device_id=(right, c), device_id_type=MESH,
        ).wait_recv()

    def mover(buf, sems, pitch, first, parts):
        def block(s, h=None):
            at = first + (0 if h != 1 else parts[0])
            return buf.at[pl.ds(s * pitch + at, sum(parts) if h is None else parts[h])]

        def push(s, row, h=None):
            copy(block(s, h), block(s, h), sems.at[s, h or 0], row)

        def wait(s, h=None):
            arrived(block(s, h), sems.at[s, h or 0])

        return push, wait

    movers = {
        "a": mover(all_p, recv_a, 4, 0, (1, 1)),
        "b": mover(all_p, recv_b, 4, 2, (1, 1)),
        "q": mover(all_q, recv_q, 8, 0, (4, 3)),
    }

    def ring(name, dz, k):
        push, wait = movers[name]
        if k == 4:
            wait(slot(dz, 4), 0)
            wait(slot(dz, 4), 1)
            return
        wait(slot(dz, -k))
        push(slot(dz, -k), right, 0 if k == 3 else None)
        wait(slot(dz, k))
        push(slot(dz, k), left, 1 if k == 3 else None)

    def turn(name, dy):
        push, wait = movers[name]
        wait(slot(3, dy))
        push(slot(3, dy), up, 0)
        wait(slot(1, dy))
        push(slot(1, dy), down, 1)

    def geo_z(d):
        return pltpu.make_async_remote_copy(
            src_ref=geo, dst_ref=col_geo.at[y, zh],
            send_sem=geo_send.at[d], recv_sem=geo_recv.at[d],
            device_id=(slot(d, 0), c), device_id_type=MESH,
        )

    def geo_y(k, way):
        place = (y - k) % N_Y if way == 0 else (y + k) % N_Y
        return pltpu.make_async_remote_copy(
            src_ref=col_geo.at[place], dst_ref=col_geo.at[place],
            send_sem=ring_send.at[way, k], recv_sem=ring_recv.at[way, k],
            device_id=(right if way == 0 else left, c), device_id_type=MESH,
        )

    def geo_y_wait(k, way):
        place = (y - k - 1) % N_Y if way == 0 else (y + k + 1) % N_Y
        arrived(col_geo.at[place], ring_recv.at[way, k])

    def geo_row(d):
        return pltpu.make_async_remote_copy(
            src_ref=geo, dst_ref=row_geo.at[c],
            send_sem=row_sems.at[0, d], recv_sem=row_sems.at[1, d],
            device_id=(r, (c + d) % N_COL), device_id_type=MESH,
        )

    def sib_copy(near, d):
        src, dst, at = (near_out, near_sib, 0) if near else (far_out, far_sib, 2)
        return pltpu.make_async_remote_copy(
            src_ref=src.at[d], dst_ref=dst.at[d],
            send_sem=sib_sems.at[at, d], recv_sem=sib_sems.at[at + 1, d],
            device_id=(r, sibling), device_id_type=MESH,
        )

    def chip_copy(near, d):
        src, dst, at = (near_sum, near_in, 0) if near else (far_sum, far_in, 2)
        return pltpu.make_async_remote_copy(
            src_ref=src.at[d], dst_ref=dst.at[d],
            send_sem=sems.at[at, d], recv_sem=sems.at[at + 1, d],
            device_id=(r, ((chip + d) % 8) * 2 + core), device_id_type=MESH,
        )

    def near_leaf(owner, k):
        return near_c[near_last[owner * 4 + k]]

    def far_whole(owner):
        parts = [far_c[far_last[owner * 7 + j]] for j in range(7)] + [jnp.zeros((64, 64), F32)]
        return jnp.concatenate(parts, axis=1)

    def event(e):
        if e == "g0":
            for d in (1, 2, 3):
                geo_z(d).start()

            @pl.loop(1, N_COL)
            def _(d):
                geo_row(d).start()

            send_later(1, 4, geo_z)
            send_later(1, N_COL, geo_row)

        elif e == "up":
            packet = upward_packet(probes_t[...], basis_t[...], moves_t[...])
            for j in range(7):
                rows = slice((j % 2) * 32, (j % 2) * 32 + 32)
                all_q[me * 8 + j] = packet[rows, (j // 2) * 128 : (j // 2) * 128 + 128]
        elif e in ("a0", "b0", "q0"):
            for row in (right, left, up, down) if e == "b0" else (up, down, right, left):
                movers[e[0]][0](me, row)
        elif e == "gz":
            for d in (1, 2, 3):
                arrived(col_geo.at[y, (zh - d) % N_ZH], geo_recv.at[d])
            geo_y(0, 0).start()
            geo_y(0, 1).start()
            send_later(0, 4, lambda k: geo_y(k, 0))
            send_later(0, 3, lambda k: geo_y(k, 1))
        elif e in ("gy1", "gy2", "gy3", "gy4"):
            k = int(e[2])
            geo_y_wait(k - 1, 0)
            if k < 4:
                geo_y(k, 0).start()
                geo_y_wait(k - 1, 1)
                if k < 3:
                    geo_y(k, 1).start()
        elif e in ("az1", "qz1"):
            turn(e[0], 0)
            for dz in (3, 1):
                movers[e[0]][0](slot(dz, 0), right)
                movers[e[0]][0](slot(dz, 0), left)
        elif e in ("az2", "qz2"):
            push, wait = movers[e[0]]
            wait(slot(2, 0), 0)
            wait(slot(2, 0), 1)
            push(slot(2, 0), right)
            push(slot(2, 0), left)
        elif e[0] in "aq":
            ring(e[0], int(e[2]), int(e[1]))
        elif e[:2] == "by":
            k = int(e[2])
            ring("b", 0, k)
            for dy in (-k, k) if k < 4 else (4,):
                movers["b"][0](slot(0, dy), up)
                movers["b"][0](slot(0, dy), down)
        elif e[:2] == "bz":
            k = int(e[2])
            for dy in (-k, k) if 0 < k < 4 else (k,):
                turn("b", dy)
        elif e == "be":
            for dy in (0, -1, 1, -2, 2, -3, 3, 4):
                movers["b"][1](slot(2, dy), 0)
                movers["b"][1](slot(2, dy), 1)
        elif e == "gr":

            @pl.loop(1, N_COL)
            def _(d):
                arrived(row_geo.at[(c + N_COL - d) % N_COL], row_sems.at[1, d])

        elif e[0] == "F":
            part = int(e[1])

            @pl.loop(part * 4, part * 4 + 4)
            def _(j):
                wide = jnp.concatenate([col_geo[j, k] for k in range(N_ZH)], axis=1)
                feat = features(sel[0:64], wide)
                for k in range(N_ZH):
                    store_features(col_leaf, col_skel, k * N_Y + j, feat[:, k * GEO : (k + 1) * GEO])

            @pl.loop(part * 2, part * 2 + 2)
            def _(j):
                wide = jnp.concatenate([row_geo[j * 4 + k] for k in range(4)], axis=1)
                feat = features(sel[64:128], wide)
                for k in range(4):
                    store_features(row_leaf, row_skel, j * 4 + k, feat[:, k * GEO : (k + 1) * GEO])

        elif e[0] == "N":
            for u in range(8):
                s = int(e[1]) * 8 + u
                square = dot_l(col_leaf[near_pair[1, s]], row_leaf[near_pair[0, s]])
                near_k[s] = matern(square).astype(BF16)
        elif e[0] == "K":

            @pl.loop(int(e[1]) * 2, int(e[1]) * 2 + 2)
            def _(g):
                for u in range(16):
                    s = g * 16 + u
                    ours = one_of(col_skel[far_pair[1, s]], far_side[2, s], far_side[3, s])
                    theirs = one_of(row_skel[far_pair[0, s]], far_side[0, s], far_side[1, s])
                    kern = matern(dot_l(ours, theirs))
                    far_k[s, 0:64] = (kern * far_side[2, s]).astype(BF16)
                    far_k[s, 64:128] = (kern * far_side[3, s]).astype(BF16)

        elif e == "U":
            far_c[0] = jnp.zeros((64, 64), F32)

            @pl.loop(0, N_ROW // 4)
            def _(g):
                for u in range(4):
                    d = g * 4 + u
                    top = all_q[d * 8 + 6]
                    all_q[d * 8 + 7] = jnp.concatenate([top[:, 64:], top[:, :64]], axis=1)

        elif e[0] == "M":

            @pl.loop(int(e[1]) * 2, int(e[1]) * 2 + 2)
            def _(g):
                for u in range(16):
                    s = g * 16 + u
                    at = far_pair[1, s] * 2
                    pair = jnp.concatenate([all_q[at], all_q[at + 1]], axis=0)
                    far_c[s + 1] = far_c[far_prev[s]] + dot_n(pair, far_k[s])

        elif e == "fs":

            @pl.loop(0, 8)
            def _(i):
                d = 7 - i
                far_out[d] = far_whole(((chip + d) % 8) * 2 + 1 - core).astype(BF16)
                sib_copy(False, d).start()

            send_later(0, 8, functools.partial(sib_copy, False))

        elif e == "fp":

            @pl.loop(0, 7)
            def _(i):
                d = 7 - i
                sib_copy(False, d).wait_recv()
                own = far_whole(((chip + d) % 8) * 2 + core)
                far_sum[d] = (own + far_sib[d].astype(F32)).astype(BF16)
                chip_copy(False, d).start()

            send_later(1, 8, functools.partial(chip_copy, False))

        elif e == "nm":
            near_c[0] = jnp.zeros((SAMPLES, LEAF), F32)

            @pl.loop(0, NEAR_MOST // 4)
            def _(g):
                for u in range(4):
                    s = g * 4 + u
                    near_c[s + 1] = near_c[near_prev[s]] + dot_n(all_p[near_pair[1, s]], near_k[s])

        elif e == "rs":

            @pl.loop(0, 8)
            def _(i):
                d = 7 - i
                owner = ((chip + d) % 8) * 2 + 1 - core
                for k in range(4):
                    near_out[d, :, k * LEAF : (k + 1) * LEAF] = near_leaf(owner, k).astype(BF16)
                sib_copy(True, d).start()

            send_later(0, 8, functools.partial(sib_copy, True))

            @pl.loop(0, 7)
            def _(i):
                d = 7 - i
                sib_copy(True, d).wait_recv()
                owner = ((chip + d) % 8) * 2 + core
                for k in range(4):
                    lanes = slice(k * LEAF, (k + 1) * LEAF)
                    theirs = near_sib[d, :, lanes].astype(F32)
                    near_sum[d, :, lanes] = (near_leaf(owner, k) + theirs).astype(BF16)
                chip_copy(True, d).start()

            send_later(1, 8, functools.partial(chip_copy, True))

        elif e == "end":
            sib_copy(False, 0).wait_recv()
            far_total = far_whole(c) + far_sib[0].astype(F32)
            for d in range(1, 8):
                chip_copy(False, d).wait_recv()
                far_total = far_total + far_in[d].astype(F32)
            top = far_total[:, 384:448]
            middle = far_total[:, 256:384] + split_dot(top, moves_t[:, 256:384])
            sib_copy(True, 0).wait_recv()
            sums = []
            for k in range(4):
                leaf = far_total[:, k * 64 : (k + 1) * 64] + split_dot(
                    middle[:, (k // 2) * 64 : (k // 2) * 64 + 64], moves_t[:, k * 64 : (k + 1) * 64]
                )
                lanes = slice(k * LEAF, (k + 1) * LEAF)
                sums.append(
                    near_leaf(c, k) + near_sib[0, :, lanes].astype(F32) + split_dot(leaf, basis_t[:, lanes])
                )
            for d in range(1, 8):
                chip_copy(True, d).wait_recv()
            for k in range(4):
                lanes = slice(k * LEAF, (k + 1) * LEAF)
                total = sums[k]
                for d in range(1, 8):
                    total = total + near_in[d, :, lanes].astype(F32)
                out[:, lanes] = total.astype(BF16)

    def store_features(leaf, skel, d, feat):
        leaf[pl.ds(d * 4, 4)] = feat[:, 0:256].reshape(4, 16, 256)
        skel[pl.ds(d * 4, 4)] = feat[:, 256:384].reshape(4, 16, 128)

    def one_of(pair, first, second):
        pair = pair.astype(F32)
        return (pair[:, :64] * first + pair[:, 64:] * second).astype(BF16)

    for e in order:
        event(e)

    for one in unsent:
        one()
    for one in sends:
        one.wait_send()


def run(chains, sel, probes_t, basis_t, moves_t, geo, order=ORDER):
    vmem = pl.BlockSpec(memory_space=pltpu.VMEM)
    smem = pl.BlockSpec(memory_space=pltpu.SMEM)
    dma = pltpu.SemaphoreType.DMA
    return pl.pallas_call(
        functools.partial(main_kernel, order),
        out_shape=jax.ShapeDtypeStruct((64, 1024), BF16),
        in_specs=[smem] * 7 + [vmem] * 5,
        out_specs=vmem,
        scratch_shapes=[
            pltpu.VMEM((4 * N_ROW, 64, LEAF), BF16),
            pltpu.VMEM((8 * N_ROW, 32, 128), BF16),
            pltpu.VMEM((N_Y, N_ZH, 16, GEO), BF16),
            pltpu.VMEM((N_COL, 16, GEO), BF16),
            pltpu.VMEM((4 * N_ROW, 16, LEAF), BF16),
            pltpu.VMEM((4 * N_COL, 16, LEAF), BF16),
            pltpu.VMEM((4 * N_ROW, 16, 128), BF16),
            pltpu.VMEM((4 * N_COL, 16, 128), BF16),
            pltpu.VMEM((NEAR_MOST, LEAF, LEAF), BF16),
            pltpu.VMEM((FAR_MOST, 2 * RANK, RANK), BF16),
            pltpu.VMEM((NEAR_MOST + 1, SAMPLES, LEAF), F32),
            pltpu.VMEM((FAR_MOST + 1, SAMPLES, RANK), F32),
            pltpu.VMEM((8, 64, 1024), BF16),
            pltpu.VMEM((8, 64, 512), BF16),
            pltpu.VMEM((8, 64, 1024), BF16),
            pltpu.VMEM((8, 64, 512), BF16),
            pltpu.VMEM((8, 64, 1024), BF16),
            pltpu.VMEM((8, 64, 512), BF16),
            pltpu.VMEM((8, 64, 1024), BF16),
            pltpu.VMEM((8, 64, 512), BF16),
            dma((120,)),
            dma((N_ROW, 2)),
            dma((N_ROW, 2)),
            dma((N_ROW, 2)),
            dma((4,)),
            dma((4,)),
            dma((2, N_COL)),
            dma((2, 4)),
            dma((2, 4)),
            dma((4, 8)),
            dma((4, 8)),
        ],
        compiler_params=pltpu.CompilerParams(
            collective_id=0, has_side_effects=True, vmem_limit_bytes=56 << 20
        ),
        name="sample",
    )(*chains, sel, probes_t, basis_t, moves_t, geo)


def local(
    probes, points, skeleton, leaf_basis, transfer, near_list, near_count, far_list, far_count
):
    probes_t, basis_t, moves_t = probes.T, leaf_basis.T, transfer.T
    sel = jnp.asarray(selections(), BF16)
    near_pairs, far_pairs = near_list[0, 0], far_list[0, 0]
    geo, *chains = prepare(near_pairs, near_count, far_pairs, far_count, points, skeleton)
    return run(chains, sel, probes_t, basis_t, moves_t, geo).T


def solution(mesh):
    placed = (
        P(("row", "col"), None),
        P(None, ("row", "col")),
        P(None, ("row", "col")),
        P(("row", "col"), None),
        P(("row", "col"), None),
        P("row", "col", None, None),
        P("row", "col"),
        P("row", "col", None, None),
        P("row", "col"),
    )
    return jax.shard_map(
        local, mesh=mesh, in_specs=placed, out_specs=P(("row", "col"), None), check_vma=False
    )
```

time: 692 us -> 108 us (0.16)
  blocking collectives: 218 us -> 0 us
  local copies, waits for them, and re-layouts: 194 us -> 1.57 us
  waiting for transfers between devices: 128 us -> 0 us
  Pallas kernels: 0 us -> 105 us
  other arithmetic: 85.3 us -> 0 us
  matrix products: 44.5 us -> 0 us
  between operations: 13.3 us -> 1.31 us
    all_gather x5 -> x0, blocking collectives: 218 us -> none  [the longest x1 75.3 us: local(): lax.all_gather(skeleton, 'row', axis=1, tiled=True)]
    gather x72 -> x0, local copies, waits for them, and re-layouts: 142 us -> none  [the longest x16 63.7 us: near_step(): col_values[sources]]
    pallas_call x0 -> x2, Pallas kernels: none -> 105 us  [the longest x1 101 us: run(): pl.pallas_call(functools.partial(main_kernel, order), out_shape=jax.Shape...]
    all_gather x3 -> x0, waiting for transfers between devices: 64.2 us -> none  [the longest x1 64.1 us: local(): lax.all_gather(leaf_basis, 'row', axis=0, tiled=True)]
    reduce_scatter x2 -> x0, waiting for transfers between devices: 61.8 us -> none  [the longest x1 61.8 us: local(): lax.psum_scatter(near_part.astype(jnp.bfloat16), 'col', scatter_dimension...]
    scatter-add x24 -> x0, other arithmetic: 58.3 us -> none  [the longest x16 36.9 us: near_step(): return totals.at[targets].add(term)]
    dot_general x30 -> x0, matrix products: 44.5 us -> none  [the longest x16 19.9 us: near_step(): jnp.einsum('gab,gbs->gas', kernel, col_values[sources], preferred_element...]
    another operation x2 -> x0, local copies, waits for them, and re-layouts: 15.8 us -> none  [the longest x1 7.9 us: upward(): basis_rows.reshape(4, LEAF, RANK)]
  transfers between devices with their start and end apart: 5 -> 0, of which waited for: 2 -> 0; matrix products, arithmetic and copies ran while one was open for 31% -> 0% of each run, Pallas kernels for 0% -> 0%
where the time goes in v2:
time: 108 us
  Pallas kernels  105 us (97%)
  local copies, waits for them, and re-layouts  1.57 us (1%)
  between operations  1.31 us (1%)
    pallas_call x1, Pallas kernels, run(): pl.pallas_call(functools.partial(main_kernel, order), out_shape=jax.Shape...  101 us
    pallas_call x1, Pallas kernels, prepare(): pl.pallas_call(prepare_kernel, out_shape=(jax.ShapeDtypeStruct((16, GEO),...  3.81 us

profile of v2, /device:TPU:1, one launch (start us, length us, event | category | flops | bytes accessed | tf_op | source)
XLA Modules:
  0.0 107.6 jit_solution(10199836268636529908)
XLA Ops:
  1.3 3.8 %prepare.1 = (bf16[16,384]{1,0:T(8,128)(2,1)}, s32[2,64]{1,0:T(2,128)}, s32[64]{0:T(128)}, s32[64]{0:T(128)}, s32[128]{0:T(128)}, /*index=5*/s32[128]{0:T(128)}, s32[2,128]{1,0:T(2,128)}, f32[4,128]{1,0:T(4,128)}) custom-call(s32[2,64]{1,0:T(2,128)} %bitcast.10, s32[1,1]{1,0:T(1,128)S(6)} %copy.12.near_count, s32[2,128]{1,0:T(2,128)} %bitcast.11, ...), custom_call_target="tpu_custom_call" | custom-call | tf_op jit(solution)/shard_map/prepare/pallas_call | solution.py:160
  5.1 100.9 %sample.1 = bf16[64,1024]{1,0:T(8,128)(2,1)} custom-call(s32[2,64]{1,0:T(2,128)} %get-tuple-element.13.near_pair, s32[64]{0:T(128)} %get-tuple-element.14.near_prev, s32[64]{0:T(128)} %get-tuple-element.15.near_last, s32[128]{0:T(128)} %get-tuple-element.16.far_prev, s32[128]{0:T(128)} %get-tuple-element.17.far_last, s32[2,128]{1,0:T(2,128)} %get-tuple-element.18.far_pair, ...), custom_call_target="tpu_custom_call" | custom-call | tf_op jit(solution)/shard_map/sample/pallas_call | solution.py:560
  106.0 1.6 %copy.14 = bf16[1024,64]{0,1:T(8,128)(2,1)} copy(bf16[1024,64]{0,1:T(8,128)(2,1)} %bitcast.6) | data formatting | bytes 262144

commit v3 on v2

--- a/solution.py
+++ b/solution.py
@@ -94,12 +94,9 @@
     return dot_n(sel, stack.astype(BF16)).astype(BF16)
 
 
-def prepare_kernel(
-    near_list, near_count, far_list, far_count, points, skeleton,
-    geo, near_pair, near_prev, near_last, far_prev, far_last, far_pair, far_side,
-):
-    pts = points[...].astype(F32)
-    skel = skeleton[...].astype(F32)
+def packed(points, skeleton):
+    pts = points.astype(F32)
+    skel = skeleton.astype(F32)
     rows = []
     for i in range(3):
         for k in range(4):
@@ -108,97 +105,70 @@
                 tail = jnp.concatenate([tail, jnp.zeros((1, 64), F32)], axis=1)
             rows.append(jnp.concatenate([pts[i : i + 1, k * LEAF : (k + 1) * LEAF], tail], axis=1))
     rows.append(jnp.zeros((4, GEO), F32))
-    geo[...] = jnp.concatenate(rows, axis=0).astype(BF16)
-
-    @pl.loop(0, FAR_MOST)
-    def _(i):
-        far_last[i] = 0
-        far_prev[i] = 0
-        for j in range(2):
-            far_pair[j, i] = 0
-            far_side[2 * j, i] = 0.0
-            far_side[2 * j + 1, i] = 0.0
-
-    @pl.loop(0, NEAR_MOST)
-    def _(i):
-        near_last[i] = 0
-        near_prev[i] = 0
-        for j in range(2):
-            near_pair[j, i] = 0
-
-    @pl.loop(0, near_count[0, 0] // 8)
-    def _(g):
-        for u in range(8):
-            s = g * 8 + u
-            a = near_list[0, s]
-            near_pair[0, s] = a
-            near_pair[1, s] = near_list[1, s]
-            near_prev[s] = near_last[a]
-            near_last[a] = s + 1
-
-    @pl.loop(0, far_count[0, 0] // 8)
-    def _(g):
-        for u in range(8):
-            s = g * 8 + u
-            a = far_list[0, s]
-            far_prev[s] = far_last[a]
-            far_last[a] = s + 1
-            for side in range(2):
-                cluster = far_list[side, s]
-                device = cluster // 7
-                local = cluster - device * 7
-                odd = (local % 2).astype(F32)
-                far_pair[side, s] = device * 4 + local // 2
-                far_side[2 * side, s] = 1.0 - odd
-                far_side[2 * side + 1, s] = odd
-
-
-def prepare(near_list, near_count, far_list, far_count, points, skeleton):
-    vmem = pl.BlockSpec(memory_space=pltpu.VMEM)
-    smem = pl.BlockSpec(memory_space=pltpu.SMEM)
-    ints = lambda *shape: jax.ShapeDtypeStruct(shape, jnp.int32)
-    return pl.pallas_call(
-        prepare_kernel,
-        out_shape=(
-            jax.ShapeDtypeStruct((16, GEO), BF16),
-            ints(2, NEAR_MOST), ints(NEAR_MOST), ints(NEAR_MOST), ints(FAR_MOST), ints(FAR_MOST), ints(2, FAR_MOST),
-            jax.ShapeDtypeStruct((4, FAR_MOST), F32),
-        ),
-        in_specs=[smem, smem, smem, smem, vmem, vmem],
-        out_specs=(vmem,) + (smem,) * 7,
-        name="prepare",
-    )(near_list, near_count, far_list, far_count, points, skeleton)
+    return jnp.concatenate(rows, axis=0).astype(BF16)
+
+
+def chain(targets, live):
+    across = jnp.broadcast_to(targets, (128, 128))
+    down = across.T
+    row = lax.broadcasted_iota(jnp.int32, (128, 128), 0)
+    lane = lax.broadcasted_iota(jnp.int32, (128, 128), 1)
+    prev = jnp.where((across == down) & (row < lane), row + 1, 0)
+    last = jnp.where((down == lane) & (row < live), row + 1, 0)
+    return jnp.max(prev, axis=0, keepdims=True), jnp.max(last, axis=0, keepdims=True)
+
+
+def slot_tables(near_list, near_live, far_list, far_live):
+    near = jnp.concatenate([near_list, jnp.zeros((2, 64), jnp.int32)], axis=1)
+    target = jnp.clip(near[0:1], 0, 4 * N_COL - 1)
+    source = jnp.clip(near[1:2], 0, 4 * N_ROW - 1)
+    far_target = jnp.clip(far_list[0:1], 0, 7 * N_COL - 1)
+    far_source = jnp.clip(far_list[1:2], 0, 7 * N_ROW - 1)
+    far = jnp.concatenate([far_target, far_source], axis=0)
+    device = (far * 9363) >> 16
+    local = far - device * 7
+    half = local >> 1
+    odd = (local - half * 2).astype(F32)
+    place = device * 4 + half
+    index = jnp.concatenate(
+        [target, source, *chain(target, near_live), place, *chain(far_target, far_live)], axis=0
+    )
+    weights = jnp.concatenate([1.0 - odd[0:1], odd[0:1], 1.0 - odd[1:2], odd[1:2]], axis=0)
+    return index, jnp.concatenate([weights, jnp.zeros((4, 128), F32)], axis=0)
 
 
 ORDER = (
-    "g0", "b0", "a0", "up", "gz", "q0", "a10", "gy1", "by1", "q10", "gy2", "qz1", "gy3", "by2", "q13", "gy4",
-    "qz2", "az1", "q11", "by3", "bz0", "gr", "F0", "q20", "q12", "a11", "F1", "bz1", "q21", "N2", "N7", "q23",
-    "N1", "az2", "q22", "by4", "q30", "a13", "K2", "N0", "N3", "K0", "q33", "K3", "q31", "N4", "q32", "q40",
-    "bz3", "a12", "a21", "K1", "q43", "N5", "q42", "a23", "bz2", "q41", "N6", "bz4", "a20", "a22", "U", "M0",
-    "a31", "M1", "a33", "M2", "a30", "M3", "a32", "fs", "a43", "a41", "be", "fp", "a42", "a40", "nm", "rs", "end",
+    "g0", "a0", "up", "q0", "gz", "b0", "a10", "q10", "gy1", "qz1", "by1", "gy2", "q13", "gr", "qz2", "bz0", "T",
+    "by2", "gy3", "q11", "q20", "q12", "az1", "gy4", "W", "F0", "by3", "F1", "q23", "q21", "K1", "q22", "N0",
+    "K0", "az2", "N4", "q30", "N5", "a11", "bz1", "N1", "q33", "q31", "bz2", "q32", "bz3", "a12", "a13", "by4",
+    "K3", "K2", "a20", "a21", "q43", "N6", "q42", "q40", "q41", "U", "M0", "a22", "M1", "a23", "M2", "M3", "a30",
+    "fs", "a31", "a32", "N3", "a33", "bz4", "xf", "N7", "N2", "a41", "a40", "a43", "a42", "na", "sa", "be", "nb",
+    "xa", "sb", "cf", "xb", "ca", "ef", "ea", "eb",
 )
 
 
 def main_kernel(
     order,
-    near_pair, near_prev, near_last, far_prev, far_last, far_pair, far_side,
-    sel, probes_t, basis_t, moves_t, geo,
+    near_count, far_count, near_list, far_list, sel, points, skeleton, probes_t, basis_t, moves_t,
     out,
-    all_p, all_q, col_geo, row_geo, col_leaf, row_leaf, col_skel, row_skel,
-    near_k, far_k, near_c, far_c, near_out, far_out,
-    near_sib, far_sib, near_sum, far_sum, near_in, far_in,
+    geo, index_v, index, weight_v, weight, table_sems,
+    all_a, all_b, all_q, col_geo, row_geo, col_leaf, row_leaf, col_skel, row_skel,
+    near_k, far_k, near_ca, near_cb, far_c, near_out, far_out,
+    near_sib, far_sib, near_sum, far_sum, near_in, far_in, far_part,
     send, recv_a, recv_b, recv_q, geo_send, geo_recv, row_sems, ring_send, ring_recv, sems, sib_sems,
 ):
     r = lax.axis_index("row")
     c = lax.axis_index("col")
-    zh = r // N_Y
-    y = r % N_Y
-    core = c % 2
-    chip = c // 2
+    zh = lax.div(r, N_Y)
+    y = lax.rem(r, N_Y)
+    core = lax.rem(c, 2)
+    chip = lax.div(c, 2)
     sibling = chip * 2 + 1 - core
+    z_lo = lax.div(chip, 4)
+    x = lax.rem(chip, 4)
 
     def slot(dz, dy):
-        return ((zh + dz) % N_ZH) * N_Y + (y + dy) % N_Y
+        return lax.rem(zh + dz, N_ZH) * N_Y + lax.rem(y + dy % N_Y, N_Y)
 
     up, down, across = slot(1, 0), slot(3, 0), slot(2, 0)
     right, left = slot(0, 1), slot(0, -1)
@@ -214,10 +184,12 @@
             barrier, inc=1, device_id=(r, (c + d) % N_COL), device_id_type=MESH
         )
 
+    geo[...] = packed(points[...], skeleton[...])
     col_geo[y, zh] = geo[...]
     row_geo[c] = geo[...]
     for k in range(4):
-        all_p[me * 4 + k] = probes_t[:, k * LEAF : (k + 1) * LEAF]
+        all_a[me * 4 + k] = probes_t[0:32, k * LEAF : (k + 1) * LEAF]
+        all_b[me * 4 + k] = probes_t[32:64, k * LEAF : (k + 1) * LEAF]
     pl.semaphore_wait(barrier, 5 + N_COL - 1)
 
     sends = []
@@ -245,9 +217,9 @@
             device_id=(right, c), device_id_type=MESH,
         ).wait_recv()
 
-    def mover(buf, sems, pitch, first, parts):
+    def mover(buf, sems, pitch, parts):
         def block(s, h=None):
-            at = first + (0 if h != 1 else parts[0])
+            at = 0 if h != 1 else parts[0]
             return buf.at[pl.ds(s * pitch + at, sum(parts) if h is None else parts[h])]
 
         def push(s, row, h=None):
@@ -259,9 +231,9 @@
         return push, wait
 
     movers = {
-        "a": mover(all_p, recv_a, 4, 0, (1, 1)),
-        "b": mover(all_p, recv_b, 4, 2, (1, 1)),
-        "q": mover(all_q, recv_q, 8, 0, (4, 3)),
+        "a": mover(all_a, recv_a, 4, (2, 2)),
+        "b": mover(all_b, recv_b, 4, (2, 2)),
+        "q": mover(all_q, recv_q, 8, (4, 3)),
     }
 
     def ring(name, dz, k):
@@ -308,28 +280,81 @@
             device_id=(r, (c + d) % N_COL), device_id_type=MESH,
         )
 
-    def sib_copy(near, d):
-        src, dst, at = (near_out, near_sib, 0) if near else (far_out, far_sib, 2)
+    outs = (near_out.at[0], near_out.at[1], far_out)
+    sibs = (near_sib.at[0], near_sib.at[1], far_sib)
+    whole = (near_sum.at[0], near_sum.at[1], far_sum)
+    comes = (near_in.at[0], near_in.at[1], far_in)
+
+    def sib_copy(what, d):
         return pltpu.make_async_remote_copy(
-            src_ref=src.at[d], dst_ref=dst.at[d],
-            send_sem=sib_sems.at[at, d], recv_sem=sib_sems.at[at + 1, d],
+            src_ref=outs[what].at[d], dst_ref=sibs[what].at[d],
+            send_sem=sib_sems.at[2 * what, d], recv_sem=sib_sems.at[2 * what + 1, d],
             device_id=(r, sibling), device_id_type=MESH,
         )
 
-    def chip_copy(near, d):
-        src, dst, at = (near_sum, near_in, 0) if near else (far_sum, far_in, 2)
+    def chip_at(d):
+        return lax.rem(z_lo + lax.div(d, 4), 2) * 4 + lax.rem(x + lax.rem(d, 4), 4)
+
+    def chip_copy(what, d, by_x=False):
+        to = chip_at(lax.rem(d, 4) if by_x else d)
         return pltpu.make_async_remote_copy(
-            src_ref=src.at[d], dst_ref=dst.at[d],
-            send_sem=sems.at[at, d], recv_sem=sems.at[at + 1, d],
-            device_id=(r, ((chip + d) % 8) * 2 + core), device_id_type=MESH,
+            src_ref=whole[what].at[d], dst_ref=comes[what].at[d],
+            send_sem=sems.at[2 * what, d], recv_sem=sems.at[2 * what + 1, d],
+            device_id=(r, to * 2 + core), device_id_type=MESH,
         )
 
-    def near_leaf(owner, k):
-        return near_c[near_last[owner * 4 + k]]
+    def core_sum(what, d):
+        sib_copy(what, d).wait_recv()
+        owner = chip_at(d) * 2 + core
+        if what == 2:
+            far_sum[d] = (far_whole(owner) + far_sib[d].astype(F32)).astype(BF16)
+            return
+        for k in range(4):
+            lanes = slice(k * LEAF, (k + 1) * LEAF)
+            theirs = near_sib[what, d, :, lanes].astype(F32)
+            near_sum[what, d, :, lanes] = (near_leaf(what, owner, k) + theirs).astype(BF16)
+
+    def spread(what):
+        @pl.loop(0, 7)
+        def _(i):
+            core_sum(what, 7 - i)
+            chip_copy(what, 7 - i).start()
+
+        send_later(1, 8, functools.partial(chip_copy, what))
+
+    def spread_x(what):
+        for first in (5, 1):
+
+            @pl.loop(0, 3)
+            def _(i):
+                d = first + 2 - i
+                core_sum(what, d)
+                chip_copy(what, d, True).start()
+
+            send_later(first, first + 3, functools.partial(chip_copy, what, by_x=True))
+
+        core_sum(what, 4)
+
+    def cross(what):
+        total = whole[what][4].astype(F32)
+        for d in (5, 6, 7):
+            chip_copy(what, d, True).wait_recv()
+            total = total + comes[what][d].astype(F32)
+        whole[what][4] = total.astype(BF16)
+        chip_copy(what, 4).start()
+        send_later(4, 5, functools.partial(chip_copy, what))
+
+    def near_leaf(h, owner, k):
+        return (near_ca, near_cb)[h][index[3, owner * 4 + k]]
 
     def far_whole(owner):
-        parts = [far_c[far_last[owner * 7 + j]] for j in range(7)] + [jnp.zeros((64, 64), F32)]
+        parts = [far_c[index[7, owner * 7 + j]] for j in range(7)] + [jnp.zeros((64, 64), F32)]
         return jnp.concatenate(parts, axis=1)
+
+    tables = (
+        pltpu.make_async_copy(index_v, index, table_sems.at[0]),
+        pltpu.make_async_copy(weight_v, weight, table_sems.at[1]),
+    )
 
     def event(e):
         if e == "g0":
@@ -419,7 +444,7 @@
         elif e[0] == "N":
             for u in range(8):
                 s = int(e[1]) * 8 + u
-                square = dot_l(col_leaf[near_pair[1, s]], row_leaf[near_pair[0, s]])
+                square = dot_l(col_leaf[index[1, s]], row_leaf[index[0, s]])
                 near_k[s] = matern(square).astype(BF16)
         elif e[0] == "K":
 
@@ -427,11 +452,11 @@
             def _(g):
                 for u in range(16):
                     s = g * 16 + u
-                    ours = one_of(col_skel[far_pair[1, s]], far_side[2, s], far_side[3, s])
-                    theirs = one_of(row_skel[far_pair[0, s]], far_side[0, s], far_side[1, s])
+                    ours = one_of(col_skel[index[5, s]], weight[2, s], weight[3, s])
+                    theirs = one_of(row_skel[index[4, s]], weight[0, s], weight[1, s])
                     kern = matern(dot_l(ours, theirs))
-                    far_k[s, 0:64] = (kern * far_side[2, s]).astype(BF16)
-                    far_k[s, 64:128] = (kern * far_side[3, s]).astype(BF16)
+                    far_k[s, 0:64] = (kern * weight[2, s]).astype(BF16)
+                    far_k[s, 64:128] = (kern * weight[3, s]).astype(BF16)
 
         elif e == "U":
             far_c[0] = jnp.zeros((64, 64), F32)
@@ -449,92 +474,85 @@
             def _(g):
                 for u in range(16):
                     s = g * 16 + u
-                    at = far_pair[1, s] * 2
+                    at = index[5, s] * 2
                     pair = jnp.concatenate([all_q[at], all_q[at + 1]], axis=0)
-                    far_c[s + 1] = far_c[far_prev[s]] + dot_n(pair, far_k[s])
+                    far_c[s + 1] = far_c[index[6, s]] + dot_n(pair, far_k[s])
 
         elif e == "fs":
 
             @pl.loop(0, 8)
             def _(i):
                 d = 7 - i
-                far_out[d] = far_whole(((chip + d) % 8) * 2 + 1 - core).astype(BF16)
-                sib_copy(False, d).start()
-
-            send_later(0, 8, functools.partial(sib_copy, False))
-
-        elif e == "fp":
-
-            @pl.loop(0, 7)
-            def _(i):
-                d = 7 - i
-                sib_copy(False, d).wait_recv()
-                own = far_whole(((chip + d) % 8) * 2 + core)
-                far_sum[d] = (own + far_sib[d].astype(F32)).astype(BF16)
-                chip_copy(False, d).start()
-
-            send_later(1, 8, functools.partial(chip_copy, False))
-
-        elif e == "nm":
-            near_c[0] = jnp.zeros((SAMPLES, LEAF), F32)
-
-            @pl.loop(0, NEAR_MOST // 4)
+                far_out[d] = far_whole(chip_at(d) * 2 + 1 - core).astype(BF16)
+                sib_copy(2, d).start()
+
+            send_later(0, 8, functools.partial(sib_copy, 2))
+
+        elif e in ("xa", "xf"):
+            spread_x(0 if e == "xa" else 2)
+        elif e in ("ca", "cf"):
+            cross(0 if e == "ca" else 2)
+        elif e == "xb":
+            spread(1)
+        elif e in ("na", "nb"):
+            sums, samples = (near_ca, all_a) if e == "na" else (near_cb, all_b)
+            sums[0] = jnp.zeros((32, LEAF), F32)
+
+            @pl.loop(0, NEAR_MOST // 16)
             def _(g):
-                for u in range(4):
-                    s = g * 4 + u
-                    near_c[s + 1] = near_c[near_prev[s]] + dot_n(all_p[near_pair[1, s]], near_k[s])
-
-        elif e == "rs":
+                for u in range(16):
+                    s = g * 16 + u
+                    sums[s + 1] = sums[index[2, s]] + dot_n(samples[index[1, s]], near_k[s])
+
+        elif e in ("sa", "sb"):
+            h = "ab".index(e[1])
 
             @pl.loop(0, 8)
             def _(i):
                 d = 7 - i
-                owner = ((chip + d) % 8) * 2 + 1 - core
+                owner = chip_at(d) * 2 + 1 - core
                 for k in range(4):
-                    near_out[d, :, k * LEAF : (k + 1) * LEAF] = near_leaf(owner, k).astype(BF16)
-                sib_copy(True, d).start()
-
-            send_later(0, 8, functools.partial(sib_copy, True))
-
-            @pl.loop(0, 7)
-            def _(i):
-                d = 7 - i
-                sib_copy(True, d).wait_recv()
-                owner = ((chip + d) % 8) * 2 + core
-                for k in range(4):
-                    lanes = slice(k * LEAF, (k + 1) * LEAF)
-                    theirs = near_sib[d, :, lanes].astype(F32)
-                    near_sum[d, :, lanes] = (near_leaf(owner, k) + theirs).astype(BF16)
-                chip_copy(True, d).start()
-
-            send_later(1, 8, functools.partial(chip_copy, True))
-
-        elif e == "end":
-            sib_copy(False, 0).wait_recv()
-            far_total = far_whole(c) + far_sib[0].astype(F32)
-            for d in range(1, 8):
-                chip_copy(False, d).wait_recv()
-                far_total = far_total + far_in[d].astype(F32)
-            top = far_total[:, 384:448]
-            middle = far_total[:, 256:384] + split_dot(top, moves_t[:, 256:384])
-            sib_copy(True, 0).wait_recv()
-            sums = []
+                    near_out[h, d, :, k * LEAF : (k + 1) * LEAF] = near_leaf(h, owner, k).astype(BF16)
+                sib_copy(h, d).start()
+
+            send_later(0, 8, functools.partial(sib_copy, h))
+        elif e == "ef":
+            sib_copy(2, 0).wait_recv()
+            total = far_whole(c) + far_sib[0].astype(F32)
+            for d in range(1, 5):
+                chip_copy(2, d).wait_recv()
+                total = total + far_in[d].astype(F32)
+            middle = total[:, 256:384] + split_dot(total[:, 384:448], moves_t[:, 256:384])
             for k in range(4):
-                leaf = far_total[:, k * 64 : (k + 1) * 64] + split_dot(
+                leaf = total[:, k * 64 : (k + 1) * 64] + split_dot(
                     middle[:, (k // 2) * 64 : (k // 2) * 64 + 64], moves_t[:, k * 64 : (k + 1) * 64]
                 )
                 lanes = slice(k * LEAF, (k + 1) * LEAF)
-                sums.append(
-                    near_leaf(c, k) + near_sib[0, :, lanes].astype(F32) + split_dot(leaf, basis_t[:, lanes])
-                )
-            for d in range(1, 8):
-                chip_copy(True, d).wait_recv()
+                far_part[:, lanes] = split_dot(leaf, basis_t[:, lanes])
+        elif e in ("ea", "eb"):
+            h = "ab".index(e[1])
+            rows = slice(32 * h, 32 * h + 32)
+            sib_copy(h, 0).wait_recv()
+            others = range(1, 5) if h == 0 else range(1, 8)
+            for d in others:
+                chip_copy(h, d).wait_recv()
             for k in range(4):
                 lanes = slice(k * LEAF, (k + 1) * LEAF)
-                total = sums[k]
-                for d in range(1, 8):
-                    total = total + near_in[d, :, lanes].astype(F32)
-                out[:, lanes] = total.astype(BF16)
+                total = near_leaf(h, c, k) + near_sib[h, 0, :, lanes].astype(F32) + far_part[rows, lanes]
+                for d in others:
+                    total = total + near_in[h, d, :, lanes].astype(F32)
+                out[rows, lanes] = total.astype(BF16)
+        elif e == "T":
+            index_v[...], weight_v[...] = slot_tables(
+                near_list[...], near_count[0, 0], far_list[...], far_count[0, 0]
+            )
+            for one in tables:
+                one.start()
+        elif e == "W":
+            for one in tables:
+                one.wait()
+        else:
+            raise ValueError(e)
 
     def store_features(leaf, skel, d, feat):
         leaf[pl.ds(d * 4, 4)] = feat[:, 0:256].reshape(4, 16, 256)
@@ -553,17 +571,24 @@
         one.wait_send()
 
 
-def run(chains, sel, probes_t, basis_t, moves_t, geo, order=ORDER):
+def run(near_count, far_count, near_list, far_list, sel, points, skeleton, probes_t, basis_t, moves_t):
     vmem = pl.BlockSpec(memory_space=pltpu.VMEM)
     smem = pl.BlockSpec(memory_space=pltpu.SMEM)
     dma = pltpu.SemaphoreType.DMA
     return pl.pallas_call(
-        functools.partial(main_kernel, order),
+        functools.partial(main_kernel, ORDER),
         out_shape=jax.ShapeDtypeStruct((64, 1024), BF16),
-        in_specs=[smem] * 7 + [vmem] * 5,
+        in_specs=[smem] * 2 + [vmem] * 8,
         out_specs=vmem,
         scratch_shapes=[
-            pltpu.VMEM((4 * N_ROW, 64, LEAF), BF16),
+            pltpu.VMEM((16, GEO), BF16),
+            pltpu.VMEM((8, 128), jnp.int32),
+            pltpu.SMEM((8, 128), jnp.int32),
+            pltpu.VMEM((8, 128), F32),
+            pltpu.SMEM((8, 128), F32),
+            dma((2,)),
+            pltpu.VMEM((4 * N_ROW, 32, LEAF), BF16),
+            pltpu.VMEM((4 * N_ROW, 32, LEAF), BF16),
             pltpu.VMEM((8 * N_ROW, 32, 128), BF16),
             pltpu.VMEM((N_Y, N_ZH, 16, GEO), BF16),
             pltpu.VMEM((N_COL, 16, GEO), BF16),
@@ -573,16 +598,18 @@
             pltpu.VMEM((4 * N_COL, 16, 128), BF16),
             pltpu.VMEM((NEAR_MOST, LEAF, LEAF), BF16),
             pltpu.VMEM((FAR_MOST, 2 * RANK, RANK), BF16),
-            pltpu.VMEM((NEAR_MOST + 1, SAMPLES, LEAF), F32),
+            pltpu.VMEM((NEAR_MOST + 1, 32, LEAF), F32),
+            pltpu.VMEM((NEAR_MOST + 1, 32, LEAF), F32),
             pltpu.VMEM((FAR_MOST + 1, SAMPLES, RANK), F32),
-            pltpu.VMEM((8, 64, 1024), BF16),
+            pltpu.VMEM((2, 8, 32, 1024), BF16),
             pltpu.VMEM((8, 64, 512), BF16),
-            pltpu.VMEM((8, 64, 1024), BF16),
+            pltpu.VMEM((2, 8, 32, 1024), BF16),
             pltpu.VMEM((8, 64, 512), BF16),
-            pltpu.VMEM((8, 64, 1024), BF16),
+            pltpu.VMEM((2, 8, 32, 1024), BF16),
             pltpu.VMEM((8, 64, 512), BF16),
-            pltpu.VMEM((8, 64, 1024), BF16),
+            pltpu.VMEM((2, 8, 32, 1024), BF16),
             pltpu.VMEM((8, 64, 512), BF16),
+            pltpu.VMEM((64, 1024), F32),
             dma((120,)),
             dma((N_ROW, 2)),
             dma((N_ROW, 2)),
@@ -592,24 +619,24 @@
             dma((2, N_COL)),
             dma((2, 4)),
             dma((2, 4)),
-            dma((4, 8)),
-            dma((4, 8)),
+            dma((6, 8)),
+            dma((6, 8)),
         ],
         compiler_params=pltpu.CompilerParams(
             collective_id=0, has_side_effects=True, vmem_limit_bytes=56 << 20
         ),
         name="sample",
-    )(*chains, sel, probes_t, basis_t, moves_t, geo)
+    )(near_count, far_count, near_list, far_list, sel, points, skeleton, probes_t, basis_t, moves_t)
 
 
 def local(
     probes, points, skeleton, leaf_basis, transfer, near_list, near_count, far_list, far_count
 ):
-    probes_t, basis_t, moves_t = probes.T, leaf_basis.T, transfer.T
     sel = jnp.asarray(selections(), BF16)
-    near_pairs, far_pairs = near_list[0, 0], far_list[0, 0]
-    geo, *chains = prepare(near_pairs, near_count, far_pairs, far_count, points, skeleton)
-    return run(chains, sel, probes_t, basis_t, moves_t, geo).T
+    return run(
+        near_count, far_count, near_list[0, 0], far_list[0, 0],
+        sel, points, skeleton, probes.T, leaf_basis.T, transfer.T,
+    ).T
 
 
 def solution(mesh):

time: 108 us -> 93 us (0.86)
  Pallas kernels: 105 us -> 90 us
    pallas_call x2 -> x1, Pallas kernels: 105 us -> 90 us  [run(): pl.pallas_call(functools.partial(main_kernel, ORDER), out_shape=jax.Shape...]
where the time goes in v3:
time: 93 us; the launch traced here: 92.9 us
  Pallas kernels  90 us (97%)
  local copies, waits for them, and re-layouts  1.57 us (2%)
  between operations  1.3 us (1%)
    pallas_call x1, Pallas kernels, run(): pl.pallas_call(functools.partial(main_kernel, ORDER), out_shape=jax.Shape...  90 us

profile of v3, /device:TPU:1, one launch (start us, length us, event | category | flops | bytes accessed | tf_op | source)
XLA Modules:
  0.0 92.9 jit_solution(8439345520761970895)
XLA Ops:
  1.3 90.0 %sample.1 = bf16[64,1024]{1,0:T(8,128)(2,1)} custom-call(s32[1,1]{1,0:T(1,128)S(6)} %copy.12.near_count, s32[1,1]{1,0:T(1,128)S(6)} %copy.13.far_count, s32[2,64]{1,0:T(2,128)} %bitcast.10, s32[2,128]{1,0:T(2,128)} %bitcast.11, bf16[128,32]{1,0:T(8,128)(2,1)} %constant.2.clone.sel, bf16[3,1024]{1,0:T(4,128)(2,1)} %points.1, bf16[3,448]{1,0:T(4,128)(2,1)} %skeleton.1, ...), custom_call_target="tpu_custom_call" | custom-call | tf_op jit(solution)/shard_map/sample/pallas_call | solution.py:578
  91.3 1.6 %copy.14 = bf16[1024,64]{0,1:T(8,128)(2,1)} copy(bf16[1024,64]{0,1:T(8,128)(2,1)} %bitcast.6) | data formatting | bytes 262144

commit v4 on v3

--- a/solution.py
+++ b/solution.py
@@ -138,19 +138,21 @@
 
 
 ORDER = (
-    "g0", "a0", "up", "q0", "gz", "b0", "a10", "q10", "gy1", "qz1", "by1", "gy2", "q13", "gr", "qz2", "bz0", "T",
-    "by2", "gy3", "q11", "q20", "q12", "az1", "gy4", "W", "F0", "by3", "F1", "q23", "q21", "K1", "q22", "N0",
-    "K0", "az2", "N4", "q30", "N5", "a11", "bz1", "N1", "q33", "q31", "bz2", "q32", "bz3", "a12", "a13", "by4",
-    "K3", "K2", "a20", "a21", "q43", "N6", "q42", "q40", "q41", "U", "M0", "a22", "M1", "a23", "M2", "M3", "a30",
-    "fs", "a31", "a32", "N3", "a33", "bz4", "xf", "N7", "N2", "a41", "a40", "a43", "a42", "na", "sa", "be", "nb",
-    "xa", "sb", "cf", "xb", "ca", "ef", "ea", "eb",
+    "a0", "pk", "g0", "b0", "a10", "up", "q0", "gz", "by1", "az1", "gy1", "qz1", "T", "by2", "gy2", "W", "q13",
+    "q10", "qz2", "by3", "gy3", "bz0", "q11", "az2", "bz1", "gr", "q12", "q20", "q23", "bz2", "gy4", "F0", "F1",
+    "q21", "K0", "K2", "q22", "K3", "a13", "N4", "a11", "N0", "q33", "q30", "q31", "N7", "N2", "q32", "by4",
+    "a12", "N6", "a20", "bz3", "a23", "K1", "a21", "q40", "q43", "q42", "q41", "U", "M0", "a22", "M1", "M2",
+    "a30", "M3", "fs", "a33", "a31", "N1", "a32", "bz4", "xf", "a40", "N5", "N3", "a43", "a42", "a41", "na", "sa",
+    "be", "nb", "sb", "xa", "cf", "xb", "sw", "ef", "ca", "ea", "eb",
 )
 
 
 def main_kernel(
     order,
-    near_count, far_count, near_list, far_list, sel, points, skeleton, probes_t, basis_t, moves_t,
-    out,
+    near_count, far_count, near_any, far_any, sel_any, points_any, skeleton_any, probes_any, basis_any,
+    moves_any,
+    out_any,
+    near_list, far_list, sel, points, skeleton, basis_t, moves_t, out, in_sems, out_sems,
     geo, index_v, index, weight_v, weight, table_sems,
     all_a, all_b, all_q, col_geo, row_geo, col_leaf, row_leaf, col_skel, row_skel,
     near_k, far_k, near_ca, near_cb, far_c, near_out, far_out,
@@ -184,15 +186,35 @@
             barrier, inc=1, device_id=(r, (c + d) % N_COL), device_id_type=MESH
         )
 
-    geo[...] = packed(points[...], skeleton[...])
-    col_geo[y, zh] = geo[...]
-    row_geo[c] = geo[...]
-    for k in range(4):
-        all_a[me * 4 + k] = probes_t[0:32, k * LEAF : (k + 1) * LEAF]
-        all_b[me * 4 + k] = probes_t[32:64, k * LEAF : (k + 1) * LEAF]
+    loads = {
+        name: pltpu.make_async_copy(src, dst, in_sems.at[i])
+        for i, (name, src, dst) in enumerate(
+            (
+                ("points", points_any, points),
+                ("skeleton", skeleton_any, skeleton),
+                ("basis", basis_any, basis_t),
+                ("moves", moves_any, moves_t),
+                ("near", near_any, near_list),
+                ("far", far_any, far_list),
+                ("sel", sel_any, sel),
+            )
+        )
+    }
+    own = []
+    for h, buf in enumerate((all_a, all_b)):
+        for k in range(4):
+            piece = probes_any.at[pl.ds(32 * h, 32), pl.ds(k * LEAF, LEAF)]
+            own.append(pltpu.make_async_copy(piece, buf.at[me * 4 + k], in_sems.at[7 + 4 * h + k]))
+    for one in own:
+        one.start()
+    for one in loads.values():
+        one.start()
+    for one in own:
+        one.wait()
     pl.semaphore_wait(barrier, 5 + N_COL - 1)
 
     sends = []
+    started = []
     unsent = []
 
     def send_later(first, last, copy_of):
@@ -205,11 +227,12 @@
 
     def copy(src, dst, sem, row):
         one = pltpu.make_async_remote_copy(
-            src_ref=src, dst_ref=dst, send_sem=send.at[len(sends)], recv_sem=sem,
+            src_ref=src, dst_ref=dst, send_sem=send.at[len(started)], recv_sem=sem,
             device_id=(row, c), device_id_type=MESH,
         )
         one.start()
         sends.append(one)
+        started.append(one)
 
     def arrived(dst, sem):
         pltpu.make_async_remote_copy(
@@ -351,13 +374,30 @@
         parts = [far_c[index[7, owner * 7 + j]] for j in range(7)] + [jnp.zeros((64, 64), F32)]
         return jnp.concatenate(parts, axis=1)
 
+    stores = [
+        pltpu.make_async_copy(
+            out.at[pl.ds(32 * h, 32)], out_any.at[pl.ds(32 * h, 32)], out_sems.at[h]
+        )
+        for h in range(2)
+    ]
     tables = (
         pltpu.make_async_copy(index_v, index, table_sems.at[0]),
         pltpu.make_async_copy(weight_v, weight, table_sems.at[1]),
     )
 
     def event(e):
-        if e == "g0":
+        if e == "pk":
+            loads["points"].wait()
+            loads["skeleton"].wait()
+            geo[...] = packed(points[...], skeleton[...])
+            col_geo[y, zh] = geo[...]
+            row_geo[c] = geo[...]
+        elif e == "sw":
+            while sends:
+                sends.pop().wait_send()
+            while unsent:
+                unsent.pop()()
+        elif e == "g0":
             for d in (1, 2, 3):
                 geo_z(d).start()
 
@@ -369,7 +409,16 @@
             send_later(1, N_COL, geo_row)
 
         elif e == "up":
-            packet = upward_packet(probes_t[...], basis_t[...], moves_t[...])
+            loads["basis"].wait()
+            loads["moves"].wait()
+            probes_t = jnp.concatenate(
+                [
+                    jnp.concatenate([buf[me * 4 + k] for k in range(4)], axis=1)
+                    for buf in (all_a, all_b)
+                ],
+                axis=0,
+            )
+            packet = upward_packet(probes_t, basis_t[...], moves_t[...])
             for j in range(7):
                 rows = slice((j % 2) * 32, (j % 2) * 32 + 32)
                 all_q[me * 8 + j] = packet[rows, (j // 2) * 128 : (j // 2) * 128 + 128]
@@ -426,6 +475,8 @@
 
         elif e[0] == "F":
             part = int(e[1])
+            if part == 0:
+                loads["sel"].wait()
 
             @pl.loop(part * 4, part * 4 + 4)
             def _(j):
@@ -542,7 +593,10 @@
                 for d in others:
                     total = total + near_in[h, d, :, lanes].astype(F32)
                 out[rows, lanes] = total.astype(BF16)
+            stores[h].start()
         elif e == "T":
+            loads["near"].wait()
+            loads["far"].wait()
             index_v[...], weight_v[...] = slot_tables(
                 near_list[...], near_count[0, 0], far_list[...], far_count[0, 0]
             )
@@ -565,22 +619,30 @@
     for e in order:
         event(e)
 
-    for one in unsent:
-        one()
-    for one in sends:
-        one.wait_send()
+    event("sw")
+    for one in stores:
+        one.wait()
 
 
 def run(near_count, far_count, near_list, far_list, sel, points, skeleton, probes_t, basis_t, moves_t):
-    vmem = pl.BlockSpec(memory_space=pltpu.VMEM)
     smem = pl.BlockSpec(memory_space=pltpu.SMEM)
     dma = pltpu.SemaphoreType.DMA
     return pl.pallas_call(
         functools.partial(main_kernel, ORDER),
         out_shape=jax.ShapeDtypeStruct((64, 1024), BF16),
-        in_specs=[smem] * 2 + [vmem] * 8,
-        out_specs=vmem,
+        in_specs=[smem] * 2 + [pl.BlockSpec(memory_space=pl.ANY)] * 8,
+        out_specs=pl.BlockSpec(memory_space=pl.ANY),
         scratch_shapes=[
+            pltpu.VMEM((2, NEAR_MOST), jnp.int32),
+            pltpu.VMEM((2, FAR_MOST), jnp.int32),
+            pltpu.VMEM((128, 32), BF16),
+            pltpu.VMEM((3, 4 * LEAF), BF16),
+            pltpu.VMEM((3, 7 * RANK), BF16),
+            pltpu.VMEM((64, 4 * LEAF), BF16),
+            pltpu.VMEM((64, 6 * RANK), BF16),
+            pltpu.VMEM((64, 4 * LEAF), BF16),
+            dma((15,)),
+            dma((2,)),
             pltpu.VMEM((16, GEO), BF16),
             pltpu.VMEM((8, 128), jnp.int32),
             pltpu.SMEM((8, 128), jnp.int32),

time: 93 us -> 98.8 us (1.062)
  Pallas kernels: 90 us -> 95.4 us
    pallas_call x1, Pallas kernels: 90 us -> 95.4 us  [run(): pl.pallas_call(functools.partial(main_kernel, ORDER), out_shape=jax.Shape...]
where the time goes in v4:
time: 98.8 us; the launch traced here: 98.2 us
  Pallas kernels  95.4 us (97%)
  local copies, waits for them, and re-layouts  1.57 us (2%)
  between operations  1.3 us (1%)
    pallas_call x1, Pallas kernels, run(): pl.pallas_call(functools.partial(main_kernel, ORDER), out_shape=jax.Shape...  95.4 us

profile of v4, /device:TPU:1, one launch (start us, length us, event | category | flops | bytes accessed | tf_op | source)
XLA Modules:
  0.0 98.2 jit_solution(17703789318735069080)
XLA Ops:
  1.3 95.4 %sample.1 = bf16[64,1024]{1,0:T(8,128)(2,1)} custom-call(s32[1,1]{1,0:T(1,128)S(6)} %copy.12.near_count, s32[1,1]{1,0:T(1,128)S(6)} %copy.13.far_count, s32[2,64]{1,0:T(2,128)} %bitcast.10, s32[2,128]{1,0:T(2,128)} %bitcast.11, bf16[128,32]{1,0:T(8,128)(2,1)} %constant.2.clone.sel_any, bf16[3,1024]{1,0:T(4,128)(2,1)} %points_any.1, ...), custom_call_target="tpu_custom_call" | custom-call | tf_op jit(solution)/shard_map/sample/pallas_call | solution.py:630
  96.7 1.6 %copy.14 = bf16[1024,64]{0,1:T(8,128)(2,1)} copy(bf16[1024,64]{0,1:T(8,128)(2,1)} %bitcast.6) | data formatting | bytes 262144

commit v5 on v4

--- a/solution.py
+++ b/solution.py
@@ -138,12 +138,12 @@
 
 
 ORDER = (
-    "a0", "pk", "g0", "b0", "a10", "up", "q0", "gz", "by1", "az1", "gy1", "qz1", "T", "by2", "gy2", "W", "q13",
-    "q10", "qz2", "by3", "gy3", "bz0", "q11", "az2", "bz1", "gr", "q12", "q20", "q23", "bz2", "gy4", "F0", "F1",
-    "q21", "K0", "K2", "q22", "K3", "a13", "N4", "a11", "N0", "q33", "q30", "q31", "N7", "N2", "q32", "by4",
-    "a12", "N6", "a20", "bz3", "a23", "K1", "a21", "q40", "q43", "q42", "q41", "U", "M0", "a22", "M1", "M2",
-    "a30", "M3", "fs", "a33", "a31", "N1", "a32", "bz4", "xf", "a40", "N5", "N3", "a43", "a42", "a41", "na", "sa",
-    "be", "nb", "sb", "xa", "cf", "xb", "sw", "ef", "ca", "ea", "eb",
+    "pk", "g0", "a0", "b0", "up", "q0", "gz", "a10", "q10", "gy1", "qz1", "by1", "gy2", "q13", "gr", "qz2", "bz0",
+    "T", "by2", "gy3", "q11", "q20", "q12", "az1", "gy4", "W", "F0", "by3", "F1", "q23", "q21", "K1", "q22", "N0",
+    "K0", "az2", "N4", "q30", "N5", "a11", "bz1", "N1", "q33", "q31", "bz2", "q32", "bz3", "a12", "a13", "by4",
+    "K3", "K2", "a20", "a21", "q43", "N6", "q42", "q40", "q41", "U", "M0", "a22", "M1", "a23", "M2", "M3", "a30",
+    "fs", "a31", "a32", "N3", "a33", "bz4", "xf", "N7", "N2", "a41", "a40", "a43", "a42", "na", "sa", "be", "nb",
+    "xa", "sb", "cf", "xb", "ca", "sw", "ef", "ea", "eb",
 )
 
 
@@ -216,14 +216,15 @@
     sends = []
     started = []
     unsent = []
-
-    def send_later(first, last, copy_of):
+    gathered = []
+
+    def send_later(first, last, copy_of, held=unsent):
         def waits():
             @pl.loop(first, last)
             def _(d):
                 copy_of(d).wait_send()
 
-        unsent.append(waits)
+        held.append(waits)
 
     def copy(src, dst, sem, row):
         one = pltpu.make_async_remote_copy(
@@ -395,8 +396,8 @@
         elif e == "sw":
             while sends:
                 sends.pop().wait_send()
-            while unsent:
-                unsent.pop()()
+            while gathered:
+                gathered.pop()()
         elif e == "g0":
             for d in (1, 2, 3):
                 geo_z(d).start()
@@ -405,8 +406,8 @@
             def _(d):
                 geo_row(d).start()
 
-            send_later(1, 4, geo_z)
-            send_later(1, N_COL, geo_row)
+            send_later(1, 4, geo_z, gathered)
+            send_later(1, N_COL, geo_row, gathered)
 
         elif e == "up":
             loads["basis"].wait()
@@ -430,8 +431,8 @@
                 arrived(col_geo.at[y, (zh - d) % N_ZH], geo_recv.at[d])
             geo_y(0, 0).start()
             geo_y(0, 1).start()
-            send_later(0, 4, lambda k: geo_y(k, 0))
-            send_later(0, 3, lambda k: geo_y(k, 1))
+            send_later(0, 4, lambda k: geo_y(k, 0), gathered)
+            send_later(0, 3, lambda k: geo_y(k, 1), gathered)
         elif e in ("gy1", "gy2", "gy3", "gy4"):
             k = int(e[2])
             geo_y_wait(k - 1, 0)
@@ -619,7 +620,8 @@
     for e in order:
         event(e)
 
-    event("sw")
+    for one in unsent:
+        one()
     for one in stores:
         one.wait()
 

time: 98.8 us -> 93.1 us (0.942)
  Pallas kernels: 95.4 us -> 90.1 us
    pallas_call x1, Pallas kernels: 95.4 us -> 90.1 us  [run(): pl.pallas_call(functools.partial(main_kernel, ORDER), out_shape=jax.Shape...]
where the time goes in v5:
time: 93.1 us; the launch traced here: 92.9 us
  Pallas kernels  90.1 us (97%)
  local copies, waits for them, and re-layouts  1.57 us (2%)
  between operations  1.3 us (1%)
    pallas_call x1, Pallas kernels, run(): pl.pallas_call(functools.partial(main_kernel, ORDER), out_shape=jax.Shape...  90.1 us

profile of v5, /device:TPU:1, one launch (start us, length us, event | category | flops | bytes accessed | tf_op | source)
XLA Modules:
  0.0 92.9 jit_solution(7324504808495772202)
XLA Ops:
  1.3 90.1 %sample.1 = bf16[64,1024]{1,0:T(8,128)(2,1)} custom-call(s32[1,1]{1,0:T(1,128)S(6)} %copy.12.near_count, s32[1,1]{1,0:T(1,128)S(6)} %copy.13.far_count, s32[2,64]{1,0:T(2,128)} %bitcast.10, s32[2,128]{1,0:T(2,128)} %bitcast.11, bf16[128,32]{1,0:T(8,128)(2,1)} %constant.2.clone.sel_any, bf16[3,1024]{1,0:T(4,128)(2,1)} %points_any.1, ...), custom_call_target="tpu_custom_call" | custom-call | tf_op jit(solution)/shard_map/sample/pallas_call | solution.py:632
  91.4 1.6 %copy.14 = bf16[1024,64]{0,1:T(8,128)(2,1)} copy(bf16[1024,64]{0,1:T(8,128)(2,1)} %bitcast.6) | data formatting | bytes 262144

commit v6 on v5

--- a/solution.py
+++ b/solution.py
@@ -140,9 +140,9 @@
 ORDER = (
     "pk", "g0", "a0", "b0", "up", "q0", "gz", "a10", "q10", "gy1", "qz1", "by1", "gy2", "q13", "gr", "qz2", "bz0",
     "T", "by2", "gy3", "q11", "q20", "q12", "az1", "gy4", "W", "F0", "by3", "F1", "q23", "q21", "K1", "q22", "N0",
-    "K0", "az2", "N4", "q30", "N5", "a11", "bz1", "N1", "q33", "q31", "bz2", "q32", "bz3", "a12", "a13", "by4",
-    "K3", "K2", "a20", "a21", "q43", "N6", "q42", "q40", "q41", "U", "M0", "a22", "M1", "a23", "M2", "M3", "a30",
-    "fs", "a31", "a32", "N3", "a33", "bz4", "xf", "N7", "N2", "a41", "a40", "a43", "a42", "na", "sa", "be", "nb",
+    "K0", "az2", "N7", "N4", "q30", "N5", "a11", "bz1", "N1", "N3", "q33", "q31", "bz2", "q32", "bz3", "a12",
+    "a13", "by4", "K3", "K2", "a20", "a21", "q43", "N6", "q42", "q40", "q41", "U", "M0", "a22", "M1", "a23", "M2",
+    "M3", "a30", "fs", "a31", "xf", "a32", "a33", "bz4", "N2", "a41", "a40", "a43", "a42", "na", "sa", "be", "nb",
     "xa", "sb", "cf", "xb", "ca", "sw", "ef", "ea", "eb",
 )
 
@@ -593,7 +593,7 @@
                 total = near_leaf(h, c, k) + near_sib[h, 0, :, lanes].astype(F32) + far_part[rows, lanes]
                 for d in others:
                     total = total + near_in[h, d, :, lanes].astype(F32)
-                out[rows, lanes] = total.astype(BF16)
+                out[rows, lanes] = total
             stores[h].start()
         elif e == "T":
             loads["near"].wait()
@@ -631,7 +631,7 @@
     dma = pltpu.SemaphoreType.DMA
     return pl.pallas_call(
         functools.partial(main_kernel, ORDER),
-        out_shape=jax.ShapeDtypeStruct((64, 1024), BF16),
+        out_shape=jax.ShapeDtypeStruct((64, 1024), F32),
         in_specs=[smem] * 2 + [pl.BlockSpec(memory_space=pl.ANY)] * 8,
         out_specs=pl.BlockSpec(memory_space=pl.ANY),
         scratch_shapes=[
@@ -642,7 +642,7 @@
             pltpu.VMEM((3, 7 * RANK), BF16),
             pltpu.VMEM((64, 4 * LEAF), BF16),
             pltpu.VMEM((64, 6 * RANK), BF16),
-            pltpu.VMEM((64, 4 * LEAF), BF16),
+            pltpu.VMEM((64, 4 * LEAF), F32),
             dma((15,)),
             dma((2,)),
             pltpu.VMEM((16, GEO), BF16),
@@ -700,7 +700,7 @@
     return run(
         near_count, far_count, near_list[0, 0], far_list[0, 0],
         sel, points, skeleton, probes.T, leaf_basis.T, transfer.T,
-    ).T
+    ).astype(BF16).T
 
 
 def solution(mesh):

time: 93.1 us -> 93.2 us (level)
  other arithmetic: 0 us -> 1.62 us
  local copies, waits for them, and re-layouts: 1.57 us -> 0 us
    transpose x0 -> x1, other arithmetic: none -> 1.62 us  [local(): return run(near_count, far_count, near_list[0, 0], far_list[0, 0], sel, p...]
    unnamed x1 -> x0, local copies, waits for them, and re-layouts: 1.57 us -> none
where the time goes in v6:
time: 93.2 us; the launch traced here: 93 us
  Pallas kernels  90.1 us (97%)
  other arithmetic  1.62 us (2%)
  between operations  1.3 us (1%)
    pallas_call x1, Pallas kernels, run(): pl.pallas_call(functools.partial(main_kernel, ORDER), out_shape=jax.Shape...  90.1 us

profile of v6, /device:TPU:1, one launch (start us, length us, event | category | flops | bytes accessed | tf_op | source)
XLA Modules:
  0.0 93.0 jit_solution(18387805461046080631)
XLA Ops:
  1.3 90.1 %sample.1 = f32[64,1024]{1,0:T(8,128)} custom-call(s32[1,1]{1,0:T(1,128)S(6)} %copy.11.near_count, s32[1,1]{1,0:T(1,128)S(6)} %copy.12.far_count, s32[2,64]{1,0:T(2,128)} %bitcast.10, s32[2,128]{1,0:T(2,128)} %bitcast.11, bf16[128,32]{1,0:T(8,128)(2,1)} %constant.2.clone.sel_any, bf16[3,1024]{1,0:T(4,128)(2,1)} %points_any.1, bf16[3,448]{1,0:T(4,128)(2,1)} %skeleton_any.1, ...), custom_call_target="tpu_custom_call" | custom-call | tf_op jit(solution)/shard_map/sample/pallas_call | solution.py:632
  91.4 1.6 %convert_bitcast_fusion = bf16[1024,64]{0,1:T(8,128)(2,1)} fusion(f32[64,1024]{1,0:T(8,128)} %sample.1), kind=kLoop, calls=%fused_computation | loop fusion | flops 65536 | bytes 393216 | tf_op jit(solution)/shard_map/transpose | solution.py:703
